TPU v7x, 32 devices: a whole 2x2x4 slice. The times are simulated.
32 devices in a mesh: parts: 2 (over y), owner: 16 (over z, x, core).
Axes of the slice: x: 2, y: 2, z: 4, core: 2. Of those that a mesh axis runs over, the one named last changes fastest.
Arguments:
- embeds: bfloat16 [8192, 1024], P(('parts', 'owner')), parts along dimension 0
- cluster: int32 [8192], P(('parts', 'owner')), parts along dimension 0, may hold values from 0 to 63, as said below
- order: int32 [8192], P(('parts', 'owner')), parts along dimension 0, may hold values from 0 to 4095, as said below
Outputs:
- nearest: float32 [8192], P(('parts', 'owner')), parts along dimension 0
There are 2 independent parts, one for each index of `parts`. A program takes and returns all parts, laid end to end along the dimension named above; each array names one. Nothing has to cross between parts.
Inputs may be any that keep to these rules, and one draw needn't show every extreme that they name: Cluster c belongs to owner c // 4. The rows of one device hold at most 32 rows of one owner's clusters; in every draw some owner gets exactly 32 from every device. A cluster has at most 128 rows, and some cluster has exactly 128. `order`: each value occurs once.
All inputs are finite; a program needn't handle non-finite values.
Results may differ from a plain program's by a relative error of at most 0.0003.
Values may be sent and summed in bfloat16 or wider, within the bound.
No kernel may reach another device: no remote copies, remote signals or barrier semaphores. Data moves between devices by JAX's collectives and lax.ppermute only.
A program may use at most 64 MiB of HBM per device.

v0:
```python
import jax
import jax.numpy as jnp
from jax import lax
from jax.sharding import PartitionSpec as P

CL_DEV = 4


def row_scales(values, width):
    squares = jnp.einsum("sd,sd->s", values, values, preferred_element_type=jnp.float32)
    return lax.rsqrt(squares / width + 1e-06)


def per_device(embeds, cluster, order):
    width = embeds.shape[1]
    count = embeds.shape[0]
    peers = lax.axis_size("owner")
    slots_each = 2 * count // peers
    total = peers * slots_each
    dest = cluster // CL_DEV
    onehot = (dest[:, None] == jnp.arange(peers, dtype=jnp.int32)[None, :]).astype(jnp.int32)
    rank = jnp.sum((jnp.cumsum(onehot, axis=0) - onehot) * onehot, axis=1)
    slot = dest * slots_each + rank
    source = jnp.full((total,), -1, jnp.int32).at[slot].set(jnp.arange(count, dtype=jnp.int32))
    filled = source >= 0
    safe = jnp.maximum(source, 0)
    outgoing = jnp.where(filled[:, None], embeds[safe], jnp.zeros((), jnp.bfloat16))
    labels = jnp.stack([jnp.where(filled, cluster[safe], -1), jnp.where(filled, order[safe], -1)])
    arrived = lax.all_to_all(outgoing, "owner", split_axis=0, concat_axis=0, tiled=True)
    tags = lax.all_to_all(labels, "owner", split_axis=1, concat_axis=1, tiled=True)
    scale = row_scales(arrived, width)
    groups = tags[0]
    orders = tags[1]
    block = min(512, total)
    nblocks = total // block

    def one_block(pieces):
        rows_blk, scale_blk, group_blk, order_blk = pieces
        gram = lax.dot_general(
            rows_blk, arrived, (((1,), (1,)), ((), ())), preferred_element_type=jnp.float32
        )
        cosine = gram * scale_blk[:, None] * scale[None, :] / width
        usable = (
            (group_blk[:, None] == groups[None, :])
            & (orders[None, :] < order_blk[:, None])
            & (groups[None, :] >= 0)
        )
        return jnp.max(jnp.where(usable, cosine, -1.0), axis=1)

    best = lax.map(
        one_block,
        (
            arrived.reshape(nblocks, block, width),
            scale.reshape(nblocks, block),
            groups.reshape(nblocks, block),
            orders.reshape(nblocks, block),
        ),
    ).reshape(total)
    returned = lax.all_to_all(best, "owner", split_axis=0, concat_axis=0, tiled=True)
    return returned[slot]


def solution(mesh):
    placed = (P(("parts", "owner"), None), P(("parts", "owner")), P(("parts", "owner")))
    return jax.shard_map(
        per_device, mesh=mesh, in_specs=placed, out_specs=P(("parts", "owner")), check_vma=False
    )
```

profile of v0, /device:TPU:0, one launch (start us, length us, event | category | flops | bytes accessed | tf_op | source)
XLA Modules:
  0.0 71.7 jit_solution(6398943894340713681)
XLA Ops:
  0.0 0.0 copy-start
  0.0 0.0 copy-start.1
  0.0 0.8 %fusion.13 = s32[2,128]{1,0:T(2,128)S(1)} fusion(s32[256]{0:T(256)} %param.4), kind=kLoop, calls=%fused_computation.40 | loop fusion | flops 3840 | bytes 2048 | tf_op jit(solution)/shard_map/eq | solution.py:21
  0.8 0.7 and_select_fusion
  1.5 0.6 reduce-window.6
  2.0 0.2 slice_reduce_fusion
  2.3 0.1 fusion.7
  2.4 0.7 compare_select_fusion
  3.1 1.4 %scatter_custom_fusion = s32[512]{0:T(512)S(1)} fusion(s32[256]{0:T(256)S(1)} %compare_select_fusion, s32[256]{0:T(256)S(1)} %iota.11, s32[]{:T(128)} %constant.30.clone.1), kind=kCustom, calls=%fused_computation.38 | custom fusion | bytes 2052 | tf_op jit(solution)/shard_map/scatter | solution.py:24
  4.5 0.0 copy-done.1
  4.5 0.0 copy-start.2
  4.5 3.5 %gather_fusion = s32[512]{0:T(512)S(1)} fusion(s32[256]{0:T(256)S(1)} %copy-done.1, s32[1024]{0:T(1024)S(1)} %pad_clamp_fusion.1), kind=kCustom, calls=%fused_computation | custom fusion | bytes 6144 | tf_op jit(solution)/shard_map/gather | solution.py:28
  8.0 0.0 copy-done.2
  8.1 3.5 %gather_fusion.1 = s32[512]{0:T(512)S(1)} fusion(s32[256]{0:T(256)S(1)} %copy-done.2, s32[1024]{0:T(1024)S(1)} %pad_clamp_fusion.1), kind=kCustom, calls=%fused_computation.1 | custom fusion | bytes 6144 | tf_op jit(solution)/shard_map/gather | solution.py:28
  11.6 0.1 stack.10
  11.7 0.1 stack.9
  11.8 0.6 pad_add_fusion
  12.4 7.4 %all-to-all-start = ((s32[2,16,32]{2,0,1:T(2,128)}), s32[2,16,32]{2,0,1:T(2,128)S(1)}, u32[]{:S(2)}, u32[]{:S(2)}) async-start(s32[2,16,32]{2,0,1:T(2,128)} %pad_add_fusion), calls=%async_computation | async-start | bytes 32768 | tf_op jit(solution)/shard_map/all_to_all | solution.py:30
  19.7 0.1 broadcast_in_dim.52
  19.8 0.0 copy-done
  19.8 2.1 %gather_fusion.2 = bf16[512,1024]{1,0:T(8,128)(2,1)S(1)} fusion(bf16[256,1024]{1,0:T(8,128)(2,1)S(1)} %copy-done, s32[1024]{0:T(1024)S(1)} %pad_clamp_fusion.1), kind=kCustom, calls=%fused_computation.2 | custom fusion | bytes 2099200 | tf_op jit(solution)/shard_map/gather | solution.py:27
  21.9 1.1 %broadcast_select_fusion = bf16[16,32,1024]{2,1,0:T(8,128)(2,1)} fusion(bf16[16,32,1024]{2,1,0:T(8,128)(2,1)S(1)} %bitcast.28, pred[16,32]{1,0:T(8,128)(4,1)S(1)} %broadcast_in_dim.52), kind=kLoop, calls=%fused_computation.12 | loop fusion | flops 524288 | bytes 2097664 | tf_op jit(solution)/shard_map/jit(_where)/select_n | solution.py:27
  23.0 3.2 %all-to-all-done = s32[2,16,32]{2,0,1:T(2,128)S(1)} async-done(((s32[2,16,32]{2,0,1:T(2,128)}), s32[2,16,32]{2,0,1:T(2,128)S(1)}, u32[]{:S(2)}, u32[]{:S(2)}) %all-to-all-start) | async-done | bytes 4128 | tf_op jit(solution)/shard_map/all_to_all | solution.py:30
  26.2 3.7 %all-to-all-start.1 = ((bf16[16,32,1024]{2,1,0:T(8,128)(2,1)}), bf16[16,32,1024]{2,1,0:T(8,128)(2,1)S(1)}, u32[]{:S(2)}, u32[]{:S(2)}) async-start(bf16[16,32,1024]{2,1,0:T(8,128)(2,1)} %broadcast_select_fusion), calls=%async_computation.1 | async-start | bytes 2097152 | tf_op jit(solution)/shard_map/all_to_all | solution.py:29
  30.0 0.1 eq.52
  30.0 0.1 lt.31
  30.1 22.7 %all-to-all-done.1 = bf16[16,32,1024]{2,1,0:T(8,128)(2,1)S(1)} async-done(((bf16[16,32,1024]{2,1,0:T(8,128)(2,1)}), bf16[16,32,1024]{2,1,0:T(8,128)(2,1)S(1)}, u32[]{:S(2)}, u32[]{:S(2)}) %all-to-all-start.1) | async-done | bytes 1048608 | tf_op jit(solution)/shard_map/all_to_all | solution.py:29
  52.8 0.3 fusion
  53.1 0.9 %fusion.4 = f32[512]{0:T(512)S(1)} fusion(bf16[512,1024]{1,0:T(8,128)(2,1)S(1)} %bitcast.29, f32[512]{0:T(512)S(1)} %add_rsqrt_fusion, s32[512]{0:T(512)S(1)} %lt.31, s32[512]{0:T(512)S(1)} %eq.52, pred[512]{0:T(512)(128)(4,1)S(1)} %broadcast_compare_fusion), kind=kOutput, calls=%fused_computation.11 | convolution fusion | flops 539229696 | bytes 1057280 | tf_op jit(solution)/shard_map/while/body/eval_jaxpr/dot_general | solution.py:39
  54.0 0.7 all_to_all.21
  54.7 6.8 %all-to-all-start.2 = ((f32[16,32,1]{1,2,0:T(1,128)}), f32[16,32,1]{1,2,0:T(1,128)S(1)}, u32[]{:S(2)}, u32[]{:S(2)}) async-start(f32[16,32,1]{1,2,0:T(1,128)} %bitcast.4), calls=%async_computation.2 | async-start | bytes 16384 | tf_op jit(solution)/shard_map/all_to_all | solution.py:59
  61.5 6.4 %all-to-all-done.2 = f32[16,32,1]{1,2,0:T(1,128)S(1)} async-done(((f32[16,32,1]{1,2,0:T(1,128)}), f32[16,32,1]{1,2,0:T(1,128)S(1)}, u32[]{:S(2)}, u32[]{:S(2)}) %all-to-all-start.2) | async-done | bytes 2080 | tf_op jit(solution)/shard_map/all_to_all | solution.py:59
  67.9 0.5 broadcast.84
  68.4 0.7 reduce.15
  69.1 0.1 all_to_all.23
  69.2 2.5 %gather_fusion.3 = f32[256]{0:T(256)} fusion(f32[512]{0:T(512)S(1)} %all_to_all.23, s32[1024]{0:T(1024)S(1)} %pad_clamp_fusion), kind=kCustom, calls=%fused_computation.3 | custom fusion | bytes 3072 | tf_op jit(solution)/shard_map/gather | solution.py:60
  (12 shorter events, 0.1 us)
Async XLA Ops:
  0.0 19.8 %copy-start = (bf16[256,1024]{1,0:T(8,128)(2,1)S(1)}, bf16[256,1024]{1,0:T(8,128)(2,1)}, u32[]{:S(2)}) copy-start(bf16[256,1024]{1,0:T(8,128)(2,1)} %param.3) | copy-start | bytes 1572868
  0.0 4.5 %copy-start.1 = (s32[256]{0:T(256)S(1)}, s32[256]{0:T(256)}, u32[]{:S(2)}) copy-start(s32[256]{0:T(256)} %param.4) | copy-start | bytes 3076
  4.5 3.5 %copy-start.2 = (s32[256]{0:T(256)S(1)}, s32[256]{0:T(256)}, u32[]{:S(2)}) copy-start(s32[256]{0:T(256)} %param.5) | copy-start | bytes 3076
  12.4 13.9 %all-to-all-start = ((s32[2,16,32]{2,0,1:T(2,128)}), s32[2,16,32]{2,0,1:T(2,128)S(1)}, u32[]{:S(2)}, u32[]{:S(2)}) async-start(s32[2,16,32]{2,0,1:T(2,128)} %pad_add_fusion), calls=%async_computation | async-start | bytes 32768 | tf_op jit(solution)/shard_map/all_to_all | solution.py:30
  26.2 26.6 %all-to-all-start.1 = ((bf16[16,32,1024]{2,1,0:T(8,128)(2,1)}), bf16[16,32,1024]{2,1,0:T(8,128)(2,1)S(1)}, u32[]{:S(2)}, u32[]{:S(2)}) async-start(bf16[16,32,1024]{2,1,0:T(8,128)(2,1)} %broadcast_select_fusion), calls=%async_computation.1 | async-start | bytes 2097152 | tf_op jit(solution)/shard_map/all_to_all | solution.py:29
  54.7 13.2 %all-to-all-start.2 = ((f32[16,32,1]{1,2,0:T(1,128)}), f32[16,32,1]{1,2,0:T(1,128)S(1)}, u32[]{:S(2)}, u32[]{:S(2)}) async-start(f32[16,32,1]{1,2,0:T(1,128)} %bitcast.4), calls=%async_computation.2 | async-start | bytes 16384 | tf_op jit(solution)/shard_map/all_to_all | solution.py:59
where the time goes:
time: 72 us; the launch traced here: 71.7 us
  waiting for transfers between devices  32.3 us (45%)
  starting transfers between devices  17.8 us (25%)
  local copies, waits for them, and re-layouts  14.9 us (21%)
  other arithmetic  5.62 us (8%)
  matrix products  0.92 us (1%)
    all_to_all x1, waiting for transfers between devices, per_device(): lax.all_to_all(outgoing, 'owner', split_axis=0, concat_axis=0, tiled=True)  22.7 us
    all_to_all x1, starting transfers between devices, per_device(): lax.all_to_all(labels, 'owner', split_axis=1, concat_axis=1, tiled=True)  7.36 us
    all_to_all x1, starting transfers between devices, per_device(): lax.all_to_all(best, 'owner', split_axis=0, concat_axis=0, tiled=True)  6.81 us
    all_to_all x1, waiting for transfers between devices, per_device(): lax.all_to_all(best, 'owner', split_axis=0, concat_axis=0, tiled=True)  6.39 us
    all_to_all x1, starting transfers between devices, per_device(): lax.all_to_all(outgoing, 'owner', split_axis=0, concat_axis=0, tiled=True)  3.65 us
    gather x1, local copies, waits for them, and re-layouts, per_device(): cluster[safe]  3.51 us
    gather x1, local copies, waits for them, and re-layouts, per_device(): order[safe]  3.51 us
    all_to_all x1, waiting for transfers between devices, per_device(): lax.all_to_all(labels, 'owner', split_axis=1, concat_axis=1, tiled=True)  3.21 us
  transfers between devices with their start and end apart: 3, of which 3 were waited for; matrix products, arithmetic and copies ran while one was open for 5% of the time, Pallas kernels for 0%

commit v1 on v0

v1 whole, which is shorter than its diff:
```python
import functools

import jax
import jax.numpy as jnp
from jax import lax
from jax.experimental import pallas as pl
from jax.experimental.pallas import tpu as pltpu
from jax.sharding import PartitionSpec as P

CL_DEV = 4
LANES = 128
EMPTY = 1e9
NOBODY = 2e9
LOWEST = -3e38
STEP = 65536.0


def iota(shape, dim):
    return lax.broadcasted_iota(jnp.int32, shape, dim)


def nt(a, b):
    return lax.dot_general(a, b, (((1,), (1,)), ((), ())), preferred_element_type=jnp.float32)


def nn(a, b):
    return lax.dot_general(a, b, (((1,), (0,)), ((), ())), preferred_element_type=jnp.float32)


def pack_kernel(peers, rows, cap, shift, cl_ref, od_ref, x_ref, out_ref, route_ref):
    count = x_ref.shape[0]
    cl = cl_ref[...]
    od = od_ref[...]
    dest = cl >> shift
    group = cl & (2**shift - 1)
    mine = iota((peers, count), 0) == dest
    before = (iota((count, count), 0) < iota((count, count), 1)).astype(jnp.bfloat16)
    ahead = nn(mine.astype(jnp.bfloat16), before)
    rank = jnp.sum(jnp.where(mine, ahead, 0.0), axis=0, keepdims=True).astype(jnp.int32)
    route_ref[0:1, :] = dest
    route_ref[1:2, :] = rank
    fits = rank < cap
    slot = jnp.where(fits, dest * rows + rank, -1)
    pick = (iota((peers * rows, count), 0) == slot).astype(jnp.bfloat16)
    fields = [od >> 8, od & 255, group + 1]
    spread = jnp.concatenate(
        [jnp.where(mine, f.astype(jnp.float32), 0.0) for f in fields], axis=0
    ).astype(jnp.bfloat16)
    place = ((iota((LANES, count), 0) == rank) & fits).astype(jnp.bfloat16)
    tags = nt(spread, place).astype(jnp.bfloat16)
    tag_row = (iota((peers * rows, peers), 0) == iota((peers * rows, peers), 1) * rows + cap).astype(jnp.bfloat16)
    width = x_ref.shape[1]
    step = 2 * LANES
    for k in range(width // step):
        part = nn(pick, x_ref[:, k * step:(k + 1) * step])
        if k == 0:
            part += nn(tag_row, jnp.concatenate([tags[0:peers], tags[peers:2 * peers]], axis=1))
        if k == 1:
            part += nn(tag_row, jnp.concatenate([tags[2 * peers:], jnp.zeros((peers, LANES), jnp.bfloat16)], axis=1))
        out_ref[:, k * step:(k + 1) * step] = part.astype(jnp.bfloat16)


def best_kernel(peers, rows, cap, x_ref, best_ref):
    total, width = x_ref.shape
    gram = nt(x_ref[...], x_ref[...])
    tag_row = (iota((peers, total), 1) == iota((peers, total), 0) * rows + cap).astype(jnp.bfloat16)
    tags = nn(tag_row, x_ref[:, :4 * LANES])
    cols = iota((peers, total), 1)
    first = iota((peers, total), 0) * rows
    block = (cols >= first) & (cols < first + rows)
    position = jnp.sum(jnp.where(block, cols - first, 0), axis=0, keepdims=True)
    spread = (iota((LANES, total), 0) == position).astype(jnp.bfloat16)
    fields = jnp.concatenate([tags[:, f * LANES:(f + 1) * LANES] for f in range(3)], axis=0).astype(jnp.bfloat16)
    flat = nn(fields, spread)
    high, low, group = [
        jnp.sum(jnp.where(block, flat[f * peers:(f + 1) * peers], 0.0), axis=0, keepdims=True) for f in range(3)
    ]
    filled = group > 0.5
    key = jnp.where(filled, group * STEP + high * 256.0 + low, EMPTY)
    floor = jnp.where(filled, group * STEP, NOBODY)
    eye = iota((total, total), 0) == iota((total, total), 1)
    key_col = jnp.sum(jnp.where(eye, key, 0.0), axis=1, keepdims=True)
    diagonal = jnp.where(eye, gram, 0.0)
    scale = lax.rsqrt(jnp.sum(diagonal, axis=0, keepdims=True) / width + 1e-06)
    scale_col = lax.rsqrt(jnp.sum(diagonal, axis=1, keepdims=True) / width + 1e-06)
    usable = (key_col < key) & (key_col >= floor)
    largest = jnp.max(jnp.where(usable, gram * scale_col, LOWEST), axis=0, keepdims=True)
    best = jnp.where(largest > LOWEST, jnp.maximum(largest * scale / width, -1.0), -1.0)
    best_ref[...] = jnp.broadcast_to(best, best_ref.shape)


def take_kernel(rows, me_ref, best_ref, route_ref, out_ref):
    peers, total = best_ref.shape
    count = out_ref.shape[1]
    dest = route_ref[0:1, :]
    slot = me_ref[0] * rows + route_ref[1:2, :]
    best = best_ref[...]
    high = best.astype(jnp.bfloat16)
    rest = best - high.astype(jnp.float32)
    mid = rest.astype(jnp.bfloat16)
    low = (rest - mid.astype(jnp.float32)).astype(jnp.bfloat16)
    pick = (iota((total, count), 0) == slot).astype(jnp.bfloat16)
    found = nn(high, pick) + nn(mid, pick) + nn(low, pick)
    mine = iota((peers, count), 0) == dest
    out_ref[...] = jnp.sum(jnp.where(mine, found, 0.0), axis=0, keepdims=True)


def per_device(embeds, cluster, order):
    count, width = embeds.shape
    peers = lax.axis_size("owner")
    cap = 2 * count // peers
    rows = -(-(cap + 1) // 8) * 8
    total = peers * rows
    shift = CL_DEV.bit_length() - 1
    vmem = pl.BlockSpec(memory_space=pltpu.VMEM)
    smem = pl.BlockSpec(memory_space=pltpu.SMEM)
    params = pltpu.CompilerParams(vmem_limit_bytes=48 * 2**20)
    packed, route = pl.pallas_call(
        functools.partial(pack_kernel, peers, rows, cap, shift),
        out_shape=[
            jax.ShapeDtypeStruct((total, width), jnp.bfloat16),
            jax.ShapeDtypeStruct((2, count), jnp.int32),
        ],
        in_specs=[vmem] * 3,
        out_specs=[vmem] * 2,
        compiler_params=params,
    )(cluster.reshape(1, count), order.reshape(1, count), embeds)
    arrived = lax.all_to_all(packed.reshape(peers, rows, width), "owner", split_axis=0, concat_axis=0, tiled=True)
    best = pl.pallas_call(
        functools.partial(best_kernel, peers, rows, cap),
        out_shape=jax.ShapeDtypeStruct((peers, total), jnp.float32),
        in_specs=[vmem],
        out_specs=vmem,
        compiler_params=params,
    )(arrived.reshape(total, width))
    returned = lax.all_to_all(best, "owner", split_axis=0, concat_axis=0, tiled=True)
    me = lax.axis_index("owner").astype(jnp.int32).reshape(1)
    nearest = pl.pallas_call(
        functools.partial(take_kernel, rows),
        out_shape=jax.ShapeDtypeStruct((1, count), jnp.float32),
        in_specs=[smem, vmem, vmem],
        out_specs=vmem,
        compiler_params=params,
    )(me, returned, route)
    return nearest.reshape(count)


def solution(mesh):
    placed = (P(("parts", "owner"), None), P(("parts", "owner")), P(("parts", "owner")))
    return jax.shard_map(
        per_device, mesh=mesh, in_specs=placed, out_specs=P(("parts", "owner")), check_vma=False
    )
```

time: 72 us -> 56.3 us (0.78)
  blocking collectives: 0 us -> 38.7 us
  waiting for transfers between devices: 32.3 us -> 6.69 us
  starting transfers between devices: 17.8 us -> 3.98 us
  local copies, waits for them, and re-layouts: 14.9 us -> 3.06 us
  other arithmetic: 5.62 us -> 0 us
  Pallas kernels: 0 us -> 3.54 us
  matrix products: 0.92 us -> 0 us
    all_to_all x0 -> x1, blocking collectives: none -> 38.7 us  [per_device(): lax.all_to_all(packed.reshape(peers, rows, width), 'owner', split_axis=0,...]
    all_to_all x2 -> x0, waiting for transfers between devices: 25.9 us -> none  [the longest x1 22.7 us: per_device(): lax.all_to_all(outgoing, 'owner', split_axis=0, concat_axis=0, tiled=True)]
    gather x4 -> x0, local copies, waits for them, and re-layouts: 11.6 us -> none  [the longest x1 3.51 us: per_device(): cluster[safe]]
    all_to_all x2 -> x0, starting transfers between devices: 11 us -> none  [the longest x1 7.36 us: per_device(): lax.all_to_all(labels, 'owner', split_axis=1, concat_axis=1, tiled=True)]
    pallas_call x0 -> x3, Pallas kernels: none -> 3.54 us  [the longest x1 1.78 us: per_device(): pl.pallas_call(functools.partial(best_kernel, peers, rows, cap), out_shap...]
    all_to_all x1, starting transfers between devices: 6.81 us -> 3.98 us  [per_device(): lax.all_to_all(best, 'owner', split_axis=0, concat_axis=0, tiled=True)]
    select_n x5 -> x0, other arithmetic: 2.53 us -> none  [the longest x1 1.14 us: per_device(): jnp.where(filled[:, None], embeds[safe], jnp.zeros((), jnp.bfloat16))]
    unnamed x6 -> x7, local copies, waits for them, and re-layouts: 0.01 us -> 2.4 us
  transfers between devices with their start and end apart: 3 -> 1, of which waited for: 3 -> 1; matrix products, arithmetic and copies ran while one was open for 5% -> 0% of each run, Pallas kernels for 0% -> 0%
where the time goes in v1:
time: 56.3 us; the launch traced here: 56 us
  blocking collectives  38.7 us (69%)
  waiting for transfers between devices  6.69 us (12%)
  starting transfers between devices  3.98 us (7%)
  Pallas kernels  3.54 us (6%)
  local copies, waits for them, and re-layouts  3.06 us (5%)
    all_to_all x1, blocking collectives, per_device(): lax.all_to_all(packed.reshape(peers, rows, width), 'owner', split_axis=0,...  38.7 us
    all_to_all x1, waiting for transfers between devices, per_device(): lax.all_to_all(best, 'owner', split_axis=0, concat_axis=0, tiled=True)  6.69 us
    all_to_all x1, starting transfers between devices, per_device(): lax.all_to_all(best, 'owner', split_axis=0, concat_axis=0, tiled=True)  3.98 us
    unnamed x7, local copies, waits for them, and re-layouts  2.4 us
    pallas_call x1, Pallas kernels, per_device(): pl.pallas_call(functools.partial(best_kernel, peers, rows, cap), out_shap...  1.78 us
  transfers between devices with their start and end apart: 1, of which 1 were waited for; matrix products, arithmetic and copies ran while one was open for 0% of the time, Pallas kernels for 0%

profile of v1, /device:TPU:0, one launch (start us, length us, event | category | flops | bytes accessed | tf_op | source)
XLA Modules:
  0.0 56.0 jit_solution(12501886404789876796)
XLA Ops:
  0.0 0.0 copy-start
  0.0 1.0 %copy-done = bf16[256,1024]{1,0:T(8,128)(2,1)S(1)} copy-done((bf16[256,1024]{1,0:T(8,128)(2,1)S(1)}, bf16[256,1024]{1,0:T(8,128)(2,1)}, u32[]{:S(2)}) %copy-start) | copy-done | bytes 524312
  1.0 0.0 copy-start.1
  1.0 0.7 %copy-done.1 = s32[256]{0:T(256)S(1)} copy-done((s32[256]{0:T(256)S(1)}, s32[256]{0:T(256)}, u32[]{:S(2)}) %copy-start.1) | copy-done | bytes 1048
  1.7 0.0 copy-start.2
  1.7 0.7 %copy-done.2 = s32[256]{0:T(256)S(1)} copy-done((s32[256]{0:T(256)S(1)}, s32[256]{0:T(256)}, u32[]{:S(2)}) %copy-start.2) | copy-done | bytes 1048
  2.4 0.9 %shard_map.37 = (bf16[640,1024]{1,0:T(8,128)(2,1)S(1)}, s32[2,256]{1,0:T(2,128)S(1)}) custom-call(s32[1,256]{1,0:T(1,128)S(1)} %bitcast.14, s32[1,256]{1,0:T(1,128)S(1)} %bitcast.15, bf16[256,1024]{1,0:T(8,128)(2,1)S(1)} %copy-done), custom_call_target="tpu_custom_call" | custom-call | tf_op jit(solution)/shard_map/pallas_call | solution.py:118
  3.3 38.7 %all_to_all.16 = bf16[16,40,1024]{2,1,0:T(8,128)(2,1)S(1)} all-to-all(bf16[16,40,1024]{2,1,0:T(8,128)(2,1)S(1)} %bitcast.11), channel_id=1, replica_groups=mesh['parts'=2,'owner'=16] {'owner'}, dimensions={0} | all-to-all | bytes 2621440 | tf_op jit(solution)/shard_map/all_to_all | solution.py:128
  42.0 1.8 %shard_map.38 = f32[16,640]{1,0:T(8,128)S(1)} custom-call(bf16[640,1024]{1,0:T(8,128)(2,1)S(1)} %bitcast.10), custom_call_target="tpu_custom_call" | custom-call | tf_op jit(solution)/shard_map/pallas_call | solution.py:129
  43.8 0.7 %copy.4 = f32[16,1,640]{2,1,0:T(1,128)} copy(f32[16,1,640]{2,0,1:T(8,128)S(1)} %bitcast.13) | data formatting | bytes 81920 | tf_op jit(solution)/shard_map/all_to_all | solution.py:136
  44.5 4.0 %all-to-all-start.1 = ((f32[16,1,640]{2,1,0:T(1,128)}), f32[16,1,640]{2,1,0:T(1,128)S(1)}, u32[]{:S(2)}, u32[]{:S(2)}) async-start(f32[16,1,640]{2,1,0:T(1,128)} %copy.4), calls=%async_computation.1 | async-start | bytes 81920 | tf_op jit(solution)/shard_map/all_to_all | solution.py:136
  48.4 6.7 %all-to-all-done.1 = f32[16,1,640]{2,1,0:T(1,128)S(1)} async-done(((f32[16,1,640]{2,1,0:T(1,128)}), f32[16,1,640]{2,1,0:T(1,128)S(1)}, u32[]{:S(2)}, u32[]{:S(2)}) %all-to-all-start.1) | async-done | bytes 40992 | tf_op jit(solution)/shard_map/all_to_all | solution.py:136
  55.1 0.8 %shard_map.39 = f32[1,256]{1,0:T(1,128)} custom-call(s32[1]{0:T(128)} %bitcast.me_ref, f32[16,640]{1,0:T(8,128)S(1)} %bitcast.12, s32[2,256]{1,0:T(2,128)S(1)} %get-tuple-element.8.route_ref), custom_call_target="tpu_custom_call" | custom-call | tf_op jit(solution)/shard_map/pallas_call | solution.py:138
  (1 shorter events, 0.0 us)
Async XLA Ops:
  0.0 1.0 %copy-start = (bf16[256,1024]{1,0:T(8,128)(2,1)S(1)}, bf16[256,1024]{1,0:T(8,128)(2,1)}, u32[]{:S(2)}) copy-start(bf16[256,1024]{1,0:T(8,128)(2,1)} %x_ref.1) | copy-start | bytes 1572868
  1.0 0.7 %copy-start.1 = (s32[256]{0:T(256)S(1)}, s32[256]{0:T(256)}, u32[]{:S(2)}) copy-start(s32[256]{0:T(256)} %param.4) | copy-start | bytes 3076
  1.7 0.7 %copy-start.2 = (s32[256]{0:T(256)S(1)}, s32[256]{0:T(256)}, u32[]{:S(2)}) copy-start(s32[256]{0:T(256)} %param.5) | copy-start | bytes 3076
  44.5 10.7 %all-to-all-start.1 = ((f32[16,1,640]{2,1,0:T(1,128)}), f32[16,1,640]{2,1,0:T(1,128)S(1)}, u32[]{:S(2)}, u32[]{:S(2)}) async-start(f32[16,1,640]{2,1,0:T(1,128)} %copy.4), calls=%async_computation.1 | async-start | bytes 81920 | tf_op jit(solution)/shard_map/all_to_all | solution.py:136

commit v2 on v1

--- a/solution.py
+++ b/solution.py
@@ -13,6 +13,7 @@
 NOBODY = 2e9
 LOWEST = -3e38
 STEP = 65536.0
+PARAMS = pltpu.CompilerParams(vmem_limit_bytes=48 * 2**20)
 
 
 def iota(shape, dim):
@@ -27,12 +28,24 @@
     return lax.dot_general(a, b, (((1,), (0,)), ((), ())), preferred_element_type=jnp.float32)
 
 
-def pack_kernel(peers, rows, cap, shift, cl_ref, od_ref, x_ref, out_ref, route_ref):
+def pack_kernel(peers, rows, cap, spread_out, cl_hbm, od_hbm, x_hbm, out_ref, route_ref, cl_ref, od_ref, x_ref, sems):
+    copies = [
+        pltpu.make_async_copy(src, dst, sems.at[k])
+        for k, (src, dst) in enumerate([(cl_hbm, cl_ref), (od_hbm, od_ref), (x_hbm, x_ref)])
+    ]
+    for copy in copies:
+        copy.start()
+    copies[0].wait()
+    copies[1].wait()
     count = x_ref.shape[0]
     cl = cl_ref[...]
     od = od_ref[...]
-    dest = cl >> shift
-    group = cl & (2**shift - 1)
+    if spread_out:
+        dest = cl & (peers - 1)
+        group = cl >> (peers.bit_length() - 1)
+    else:
+        dest = cl >> (CL_DEV.bit_length() - 1)
+        group = cl & (CL_DEV - 1)
     mine = iota((peers, count), 0) == dest
     before = (iota((count, count), 0) < iota((count, count), 1)).astype(jnp.bfloat16)
     ahead = nn(mine.astype(jnp.bfloat16), before)
@@ -49,22 +62,26 @@
     place = ((iota((LANES, count), 0) == rank) & fits).astype(jnp.bfloat16)
     tags = nt(spread, place).astype(jnp.bfloat16)
     tag_row = (iota((peers * rows, peers), 0) == iota((peers * rows, peers), 1) * rows + cap).astype(jnp.bfloat16)
+    crowded = jnp.max((rank >= cap).astype(jnp.float32), axis=1, keepdims=True)
+    crowded = jnp.broadcast_to(crowded, (peers, LANES)).astype(jnp.bfloat16)
     width = x_ref.shape[1]
     step = 2 * LANES
+    copies[2].wait()
     for k in range(width // step):
         part = nn(pick, x_ref[:, k * step:(k + 1) * step])
         if k == 0:
             part += nn(tag_row, jnp.concatenate([tags[0:peers], tags[peers:2 * peers]], axis=1))
         if k == 1:
-            part += nn(tag_row, jnp.concatenate([tags[2 * peers:], jnp.zeros((peers, LANES), jnp.bfloat16)], axis=1))
+            part += nn(tag_row, jnp.concatenate([tags[2 * peers:], crowded], axis=1))
         out_ref[:, k * step:(k + 1) * step] = part.astype(jnp.bfloat16)
 
 
-def best_kernel(peers, rows, cap, x_ref, best_ref):
+def best_kernel(peers, rows, cap, x_ref, best_ref, crowded_ref):
     total, width = x_ref.shape
     gram = nt(x_ref[...], x_ref[...])
     tag_row = (iota((peers, total), 1) == iota((peers, total), 0) * rows + cap).astype(jnp.bfloat16)
     tags = nn(tag_row, x_ref[:, :4 * LANES])
+    crowded_ref[0] = jnp.max(tags[:, 3 * LANES:]).astype(jnp.int32)
     cols = iota((peers, total), 1)
     first = iota((peers, total), 0) * rows
     block = (cols >= first) & (cols < first + rows)
@@ -105,34 +122,43 @@
     out_ref[...] = jnp.sum(jnp.where(mine, found, 0.0), axis=0, keepdims=True)
 
 
-def per_device(embeds, cluster, order):
+def send(rows, cap, spread_out, embeds, cluster, order):
     count, width = embeds.shape
     peers = lax.axis_size("owner")
-    cap = 2 * count // peers
-    rows = -(-(cap + 1) // 8) * 8
     total = peers * rows
-    shift = CL_DEV.bit_length() - 1
     vmem = pl.BlockSpec(memory_space=pltpu.VMEM)
     smem = pl.BlockSpec(memory_space=pltpu.SMEM)
-    params = pltpu.CompilerParams(vmem_limit_bytes=48 * 2**20)
     packed, route = pl.pallas_call(
-        functools.partial(pack_kernel, peers, rows, cap, shift),
+        functools.partial(pack_kernel, peers, rows, cap, spread_out),
         out_shape=[
             jax.ShapeDtypeStruct((total, width), jnp.bfloat16),
             jax.ShapeDtypeStruct((2, count), jnp.int32),
         ],
-        in_specs=[vmem] * 3,
+        in_specs=[pl.BlockSpec(memory_space=pl.ANY)] * 3,
         out_specs=[vmem] * 2,
-        compiler_params=params,
+        scratch_shapes=[
+            pltpu.VMEM((1, count), jnp.int32),
+            pltpu.VMEM((1, count), jnp.int32),
+            pltpu.VMEM((count, width), jnp.bfloat16),
+            pltpu.SemaphoreType.DMA((3,)),
+        ],
+        compiler_params=PARAMS,
     )(cluster.reshape(1, count), order.reshape(1, count), embeds)
     arrived = lax.all_to_all(packed.reshape(peers, rows, width), "owner", split_axis=0, concat_axis=0, tiled=True)
-    best = pl.pallas_call(
+    best, crowded = pl.pallas_call(
         functools.partial(best_kernel, peers, rows, cap),
-        out_shape=jax.ShapeDtypeStruct((peers, total), jnp.float32),
+        out_shape=[jax.ShapeDtypeStruct((peers, total), jnp.float32), jax.ShapeDtypeStruct((1,), jnp.int32)],
         in_specs=[vmem],
-        out_specs=vmem,
-        compiler_params=params,
+        out_specs=[vmem, smem],
+        compiler_params=PARAMS,
     )(arrived.reshape(total, width))
+    return best, route, crowded
+
+
+def bring_back(rows, best, route):
+    count = route.shape[1]
+    vmem = pl.BlockSpec(memory_space=pltpu.VMEM)
+    smem = pl.BlockSpec(memory_space=pltpu.SMEM)
     returned = lax.all_to_all(best, "owner", split_axis=0, concat_axis=0, tiled=True)
     me = lax.axis_index("owner").astype(jnp.int32).reshape(1)
     nearest = pl.pallas_call(
@@ -140,9 +166,29 @@
         out_shape=jax.ShapeDtypeStruct((1, count), jnp.float32),
         in_specs=[smem, vmem, vmem],
         out_specs=vmem,
-        compiler_params=params,
+        compiler_params=PARAMS,
     )(me, returned, route)
     return nearest.reshape(count)
+
+
+def per_device(embeds, cluster, order):
+    count = embeds.shape[0]
+    most = 2 * count // lax.axis_size("owner")
+
+    def roomy(embeds, cluster, order):
+        rows = -(-(most + 1) // 8) * 8
+        best, route, _ = send(rows, most, False, embeds, cluster, order)
+        return bring_back(rows, best, route)
+
+    rows = 3 * most // 4
+    if rows % 8:
+        return roomy(embeds, cluster, order)
+    best, route, crowded = send(rows, rows - 1, True, embeds, cluster, order)
+    return lax.cond(
+        crowded[0] > 0,
+        lambda: roomy(embeds, cluster, order),
+        lambda: bring_back(rows, best, route),
+    )
 
 
 def solution(mesh):

time: 56.3 us -> 44.4 us (0.79)
  blocking collectives: 38.7 us -> 0 us
  waiting for transfers between devices: 6.69 us -> 25.3 us
  starting transfers between devices: 3.98 us -> 13 us
  local copies, waits for them, and re-layouts: 3.06 us -> 1.2 us
  between operations: 0.03 us -> 0.74 us
    all_to_all x1 -> x0, blocking collectives: 38.7 us -> none  [per_device(): lax.all_to_all(packed.reshape(peers, rows, width), 'owner', split_axis=0,...]
    all_to_all x1 -> x2, waiting for transfers between devices: 6.69 us -> 25.3 us  [the longest x1 18.7 us: send(): lax.all_to_all(packed.reshape(peers, rows, width), 'owner', split_axis=0,...]
    all_to_all x1 -> x2, starting transfers between devices: 3.98 us -> 13 us  [the longest x1 7.5 us: send(): lax.all_to_all(packed.reshape(peers, rows, width), 'owner', split_axis=0,...]
    unnamed x7 -> x8, local copies, waits for them, and re-layouts: 2.4 us -> 0.58 us
  transfers between devices with their start and end apart: 1 -> 2, of which waited for: 1 -> 2; matrix products, arithmetic and copies ran while one was open for 0% -> 0% of each run, Pallas kernels for 0% -> 0%
where the time goes in v2:
time: 44.4 us; the launch traced here: 44.1 us
  waiting for transfers between devices  25.3 us (57%)
  starting transfers between devices  13 us (29%)
  Pallas kernels  3.92 us (9%)
  local copies, waits for them, and re-layouts  1.2 us (3%)
  between operations  0.74 us (2%)
    all_to_all x1, waiting for transfers between devices, send(): lax.all_to_all(packed.reshape(peers, rows, width), 'owner', split_axis=0,...  18.7 us
    all_to_all x1, starting transfers between devices, send(): lax.all_to_all(packed.reshape(peers, rows, width), 'owner', split_axis=0,...  7.5 us
    all_to_all x1, waiting for transfers between devices, bring_back(): lax.all_to_all(best, 'owner', split_axis=0, concat_axis=0, tiled=True)  6.56 us
    all_to_all x1, starting transfers between devices, bring_back(): lax.all_to_all(best, 'owner', split_axis=0, concat_axis=0, tiled=True)  5.47 us
    pallas_call x1, Pallas kernels, send(): pl.pallas_call(functools.partial(pack_kernel, peers, rows, cap, spread_ou...  2.44 us
    pallas_call x1, Pallas kernels, send(): pl.pallas_call(functools.partial(best_kernel, peers, rows, cap), out_shap...  1.25 us
  transfers between devices with their start and end apart: 2, of which 2 were waited for; matrix products, arithmetic and copies ran while one was open for 0% of the time, Pallas kernels for 0%

profile of v2, /device:TPU:0, one launch (start us, length us, event | category | flops | bytes accessed | tf_op | source)
XLA Modules:
  0.0 44.1 jit_solution(2447252243145713366)
XLA Ops:
  0.0 2.4 %shard_map.39 = (bf16[384,1024]{1,0:T(8,128)(2,1)}, s32[2,256]{1,0:T(2,128)S(1)}) custom-call(s32[1,256]{1,0:T(1,128)} %bitcast.26, s32[1,256]{1,0:T(1,128)} %bitcast.28, bf16[256,1024]{1,0:T(8,128)(2,1)} %x_hbm.1), custom_call_target="tpu_custom_call" | custom-call | tf_op jit(solution)/shard_map/pallas_call | solution.py:131
  2.5 0.0 copy-start
  2.5 0.0 copy-start.1
  2.5 0.0 copy-start.2
  2.5 7.5 %all-to-all-start.3 = ((bf16[16,24,1024]{2,1,0:T(8,128)(2,1)}), bf16[16,24,1024]{2,1,0:T(8,128)(2,1)S(1)}, u32[]{:S(2)}, u32[]{:S(2)}) async-start(bf16[16,24,1024]{2,1,0:T(8,128)(2,1)} %bitcast.11), calls=%async_computation.3 | async-start | bytes 1572864 | tf_op jit(solution)/shard_map/all_to_all | solution.py:147
  10.0 18.7 %all-to-all-done.3 = bf16[16,24,1024]{2,1,0:T(8,128)(2,1)S(1)} async-done(((bf16[16,24,1024]{2,1,0:T(8,128)(2,1)}), bf16[16,24,1024]{2,1,0:T(8,128)(2,1)S(1)}, u32[]{:S(2)}, u32[]{:S(2)}) %all-to-all-start.3) | async-done | bytes 786464 | tf_op jit(solution)/shard_map/all_to_all | solution.py:147
  28.7 1.3 %shard_map.40 = (f32[16,384]{1,0:T(8,128)S(1)}, s32[1]{0:T(128)}) custom-call(bf16[384,1024]{1,0:T(8,128)(2,1)S(1)} %bitcast.21), custom_call_target="tpu_custom_call" | custom-call | tf_op jit(solution)/shard_map/pallas_call | solution.py:148
  30.6 0.0 copy-done
  30.6 0.0 copy-done.1
  30.6 0.0 copy-done.2
  30.6 12.9 %conditional.1 = (f32[256]{0:T(256)S(1)}) conditional(s32[]{:T(128)} %bitcast.13, (f32[16,384]{1,0:T(8,128)S(1)}, s32[2,256]{1,0:T(2,128)S(1)}) %tuple.11, (s32[256]{0:T(256)S(1)}, s32[256]{0:T(256)S(1)}, bf16[256,1024]{1,0:T(8,128)(2,1)S(1)}) %tuple.19), branch_computations={%region_0.0_spmd, %region_1.0_spmd} | conditional | flops 2 | bytes 2908220 | solution.py:187
  30.7 0.6 %all_to_all.3 = f32[16,1,384]{2,1,0:T(1,128)} reshape(f32[16,384]{1,0:T(8,128)S(1)} %get-tuple-element.18) | data formatting | bytes 49152 | tf_op jit(solution)/shard_map/cond/branch_0_fun/all_to_all | solution.py:162
  31.3 5.5 %all-to-all-start = ((f32[16,1,384]{2,1,0:T(1,128)}), f32[16,1,384]{2,1,0:T(1,128)S(1)}, u32[]{:S(2)}, u32[]{:S(2)}) async-start(f32[16,1,384]{2,1,0:T(1,128)} %all_to_all.3), calls=%async_computation | async-start | bytes 49152 | tf_op jit(solution)/shard_map/cond/branch_0_fun/all_to_all | solution.py:162
  36.8 6.6 %all-to-all-done = f32[16,1,384]{2,1,0:T(1,128)S(1)} async-done(((f32[16,1,384]{2,1,0:T(1,128)}), f32[16,1,384]{2,1,0:T(1,128)S(1)}, u32[]{:S(2)}, u32[]{:S(2)}) %all-to-all-start) | async-done | bytes 24608 | tf_op jit(solution)/shard_map/cond/branch_0_fun/all_to_all | solution.py:162
  43.3 0.2 branch_0_fun.1
  43.6 0.0 copy-start.3
  43.6 0.6 %copy-done.3 = f32[256]{0:T(256)} copy-done((f32[256]{0:T(256)}, f32[256]{0:T(256)S(1)}, u32[]{:S(2)}) %copy-start.3) | copy-done | bytes 1048
  (1 shorter events, 0.0 us)
Async XLA Ops:
  2.5 28.2 %copy-start = (bf16[256,1024]{1,0:T(8,128)(2,1)S(1)}, bf16[256,1024]{1,0:T(8,128)(2,1)}, u32[]{:S(2)}) copy-start(bf16[256,1024]{1,0:T(8,128)(2,1)} %x_hbm.1) | copy-start | bytes 1572868
  2.5 28.2 %copy-start.1 = (s32[256]{0:T(256)S(1)}, s32[256]{0:T(256)}, u32[]{:S(2)}) copy-start(s32[256]{0:T(256)} %param.6) | copy-start | bytes 3076
  2.5 28.2 %copy-start.2 = (s32[256]{0:T(256)S(1)}, s32[256]{0:T(256)}, u32[]{:S(2)}) copy-start(s32[256]{0:T(256)} %param.7) | copy-start | bytes 3076
  2.5 26.2 %all-to-all-start.3 = ((bf16[16,24,1024]{2,1,0:T(8,128)(2,1)}), bf16[16,24,1024]{2,1,0:T(8,128)(2,1)S(1)}, u32[]{:S(2)}, u32[]{:S(2)}) async-start(bf16[16,24,1024]{2,1,0:T(8,128)(2,1)} %bitcast.11), calls=%async_computation.3 | async-start | bytes 1572864 | tf_op jit(solution)/shard_map/all_to_all | solution.py:147
  31.3 12.0 %all-to-all-start = ((f32[16,1,384]{2,1,0:T(1,128)}), f32[16,1,384]{2,1,0:T(1,128)S(1)}, u32[]{:S(2)}, u32[]{:S(2)}) async-start(f32[16,1,384]{2,1,0:T(1,128)} %all_to_all.3), calls=%async_computation | async-start | bytes 49152 | tf_op jit(solution)/shard_map/cond/branch_0_fun/all_to_all | solution.py:162
  43.6 0.6 %copy-start.3 = (f32[256]{0:T(256)}, f32[256]{0:T(256)S(1)}, u32[]{:S(2)}) copy-start(f32[256]{0:T(256)S(1)} %get-tuple-element.40) | copy-start | bytes 3076

commit v3 on v2

--- a/solution.py
+++ b/solution.py
@@ -29,15 +29,17 @@
 
 
 def pack_kernel(peers, rows, cap, spread_out, cl_hbm, od_hbm, x_hbm, out_ref, route_ref, cl_ref, od_ref, x_ref, sems):
-    copies = [
-        pltpu.make_async_copy(src, dst, sems.at[k])
-        for k, (src, dst) in enumerate([(cl_hbm, cl_ref), (od_hbm, od_ref), (x_hbm, x_ref)])
-    ]
+    count, width = x_ref.shape
+    step = 2 * LANES
+    pieces = [(cl_hbm, cl_ref), (od_hbm, od_ref)]
+    for k in range(width // step):
+        columns = pl.ds(k * step, step)
+        pieces.append((x_hbm.at[:, columns], x_ref.at[:, columns]))
+    copies = [pltpu.make_async_copy(src, dst, sems.at[k]) for k, (src, dst) in enumerate(pieces)]
     for copy in copies:
         copy.start()
     copies[0].wait()
     copies[1].wait()
-    count = x_ref.shape[0]
     cl = cl_ref[...]
     od = od_ref[...]
     if spread_out:
@@ -64,10 +66,8 @@
     tag_row = (iota((peers * rows, peers), 0) == iota((peers * rows, peers), 1) * rows + cap).astype(jnp.bfloat16)
     crowded = jnp.max((rank >= cap).astype(jnp.float32), axis=1, keepdims=True)
     crowded = jnp.broadcast_to(crowded, (peers, LANES)).astype(jnp.bfloat16)
-    width = x_ref.shape[1]
-    step = 2 * LANES
-    copies[2].wait()
     for k in range(width // step):
+        copies[2 + k].wait()
         part = nn(pick, x_ref[:, k * step:(k + 1) * step])
         if k == 0:
             part += nn(tag_row, jnp.concatenate([tags[0:peers], tags[peers:2 * peers]], axis=1))
@@ -103,15 +103,15 @@
     usable = (key_col < key) & (key_col >= floor)
     largest = jnp.max(jnp.where(usable, gram * scale_col, LOWEST), axis=0, keepdims=True)
     best = jnp.where(largest > LOWEST, jnp.maximum(largest * scale / width, -1.0), -1.0)
-    best_ref[...] = jnp.broadcast_to(best, best_ref.shape)
+    best_ref[...] = jnp.broadcast_to(best[None], best_ref.shape)
 
 
 def take_kernel(rows, me_ref, best_ref, route_ref, out_ref):
-    peers, total = best_ref.shape
+    peers, _, total = best_ref.shape
     count = out_ref.shape[1]
     dest = route_ref[0:1, :]
     slot = me_ref[0] * rows + route_ref[1:2, :]
-    best = best_ref[...]
+    best = best_ref[:, 0, :]
     high = best.astype(jnp.bfloat16)
     rest = best - high.astype(jnp.float32)
     mid = rest.astype(jnp.bfloat16)
@@ -120,6 +120,17 @@
     found = nn(high, pick) + nn(mid, pick) + nn(low, pick)
     mine = iota((peers, count), 0) == dest
     out_ref[...] = jnp.sum(jnp.where(mine, found, 0.0), axis=0, keepdims=True)
+
+
+def exchange(blocks):
+    peers = blocks.shape[0]
+    group = [(k + peers // 2 + 1) % peers for k in range(peers)]
+    return lax.all_to_all(blocks, "owner", split_axis=0, concat_axis=0, tiled=True, axis_index_groups=[group])
+
+
+def place_in_group():
+    peers = lax.axis_size("owner")
+    return ((lax.axis_index("owner") + (peers - peers // 2 - 1)) % peers).astype(jnp.int32).reshape(1)
 
 
 def send(rows, cap, spread_out, embeds, cluster, order):
@@ -140,14 +151,14 @@
             pltpu.VMEM((1, count), jnp.int32),
             pltpu.VMEM((1, count), jnp.int32),
             pltpu.VMEM((count, width), jnp.bfloat16),
-            pltpu.SemaphoreType.DMA((3,)),
+            pltpu.SemaphoreType.DMA((2 + width // (2 * LANES),)),
         ],
         compiler_params=PARAMS,
     )(cluster.reshape(1, count), order.reshape(1, count), embeds)
-    arrived = lax.all_to_all(packed.reshape(peers, rows, width), "owner", split_axis=0, concat_axis=0, tiled=True)
+    arrived = exchange(packed.reshape(peers, rows, width))
     best, crowded = pl.pallas_call(
         functools.partial(best_kernel, peers, rows, cap),
-        out_shape=[jax.ShapeDtypeStruct((peers, total), jnp.float32), jax.ShapeDtypeStruct((1,), jnp.int32)],
+        out_shape=[jax.ShapeDtypeStruct((peers, 1, total), jnp.float32), jax.ShapeDtypeStruct((1,), jnp.int32)],
         in_specs=[vmem],
         out_specs=[vmem, smem],
         compiler_params=PARAMS,
@@ -155,12 +166,10 @@
     return best, route, crowded
 
 
-def bring_back(rows, best, route):
+def take(rows, me, returned, route):
     count = route.shape[1]
     vmem = pl.BlockSpec(memory_space=pltpu.VMEM)
     smem = pl.BlockSpec(memory_space=pltpu.SMEM)
-    returned = lax.all_to_all(best, "owner", split_axis=0, concat_axis=0, tiled=True)
-    me = lax.axis_index("owner").astype(jnp.int32).reshape(1)
     nearest = pl.pallas_call(
         functools.partial(take_kernel, rows),
         out_shape=jax.ShapeDtypeStruct((1, count), jnp.float32),
@@ -175,20 +184,23 @@
     count = embeds.shape[0]
     most = 2 * count // lax.axis_size("owner")
 
-    def roomy(embeds, cluster, order):
+    def roomy():
         rows = -(-(most + 1) // 8) * 8
         best, route, _ = send(rows, most, False, embeds, cluster, order)
-        return bring_back(rows, best, route)
+        return take(rows, place_in_group(), exchange(best), route)
 
     rows = 3 * most // 4
     if rows % 8:
-        return roomy(embeds, cluster, order)
+        return roomy()
     best, route, crowded = send(rows, rows - 1, True, embeds, cluster, order)
-    return lax.cond(
-        crowded[0] > 0,
-        lambda: roomy(embeds, cluster, order),
-        lambda: bring_back(rows, best, route),
-    )
+    returned = exchange(best)
+
+    def again():
+        results = jnp.zeros_like(returned).at[0, 0, :count].set(roomy())
+        places = jnp.stack([jnp.zeros((count,), jnp.int32), jnp.arange(count, dtype=jnp.int32)])
+        return jnp.zeros((1,), jnp.int32), results, places
+
+    return take(rows, *lax.cond(crowded[0] > 0, again, lambda: (place_in_group(), returned, route)))
 
 
 def solution(mesh):

time: 44.4 us -> 40 us (0.901)
  blocking collectives: 0 us -> 25.5 us
  waiting for transfers between devices: 25.3 us -> 3.63 us
  starting transfers between devices: 13 us -> 5.24 us
  local copies, waits for them, and re-layouts: 1.2 us -> 0.02 us
  Pallas kernels: 3.92 us -> 4.68 us
    all_to_all x0 -> x1, blocking collectives: none -> 25.5 us  [exchange(): lax.all_to_all(blocks, 'owner', split_axis=0, concat_axis=0, tiled=True,...]
    all_to_all x2 -> x1, waiting for transfers between devices: 25.3 us -> 3.63 us  [exchange(): lax.all_to_all(blocks, 'owner', split_axis=0, concat_axis=0, tiled=True,...]
    all_to_all x2 -> x1, starting transfers between devices: 13 us -> 5.24 us  [exchange(): lax.all_to_all(blocks, 'owner', split_axis=0, concat_axis=0, tiled=True,...]
    pallas_call x1, Pallas kernels: 0.22 us -> 0.88 us  [take(): pl.pallas_call(functools.partial(take_kernel, rows), out_shape=jax.ShapeD...]
    all_to_all x1 -> x0, local copies, waits for them, and re-layouts: 0.62 us -> none  [bring_back(): lax.all_to_all(best, 'owner', split_axis=0, concat_axis=0, tiled=True)]
    unnamed x8 -> x6, local copies, waits for them, and re-layouts: 0.58 us -> 0.02 us
  transfers between devices with their start and end apart: 2 -> 1, of which waited for: 2 -> 1; matrix products, arithmetic and copies ran while one was open for 0% -> 0% of each run, Pallas kernels for 0% -> 0%
where the time goes in v3:
time: 40 us; the launch traced here: 39.8 us
  blocking collectives  25.5 us (64%)
  starting transfers between devices  5.24 us (13%)
  Pallas kernels  4.68 us (12%)
  waiting for transfers between devices  3.63 us (9%)
  between operations  0.71 us (2%)
    all_to_all x1, blocking collectives, exchange(): lax.all_to_all(blocks, 'owner', split_axis=0, concat_axis=0, tiled=True,...  25.5 us
    all_to_all x1, starting transfers between devices, exchange(): lax.all_to_all(blocks, 'owner', split_axis=0, concat_axis=0, tiled=True,...  5.24 us
    all_to_all x1, waiting for transfers between devices, exchange(): lax.all_to_all(blocks, 'owner', split_axis=0, concat_axis=0, tiled=True,...  3.63 us
    pallas_call x1, Pallas kernels, send(): pl.pallas_call(functools.partial(pack_kernel, peers, rows, cap, spread_ou...  2.24 us
    pallas_call x1, Pallas kernels, send(): pl.pallas_call(functools.partial(best_kernel, peers, rows, cap), out_shap...  1.56 us
    pallas_call x1, Pallas kernels, take(): pl.pallas_call(functools.partial(take_kernel, rows), out_shape=jax.ShapeD...  0.88 us
  transfers between devices with their start and end apart: 1, of which 1 were waited for; matrix products, arithmetic and copies ran while one was open for 0% of the time, Pallas kernels for 0%

profile of v3, /device:TPU:0, one launch (start us, length us, event | category | flops | bytes accessed | tf_op | source)
XLA Modules:
  0.0 39.8 jit_solution(8009387216420161421)
XLA Ops:
  0.0 2.2 %shard_map.37 = (bf16[384,1024]{1,0:T(8,128)(2,1)S(1)}, s32[2,256]{1,0:T(2,128)S(1)}) custom-call(s32[1,256]{1,0:T(1,128)} %bitcast.18, s32[1,256]{1,0:T(1,128)} %bitcast.20, bf16[256,1024]{1,0:T(8,128)(2,1)} %x_hbm.1), custom_call_target="tpu_custom_call" | custom-call | tf_op jit(solution)/shard_map/pallas_call | solution.py:142
  2.3 0.0 copy-start
  2.3 0.0 copy-start.1
  2.3 0.0 copy-start.2
  2.3 25.5 %all_to_all.19 = bf16[16,24,1024]{2,1,0:T(8,128)(2,1)S(1)} all-to-all(bf16[16,24,1024]{2,1,0:T(8,128)(2,1)S(1)} %bitcast.16), channel_id=1, replica_groups={{9,10,11,12,13,14,15,0,1,2,3,4,5,6,7,8},{25,26,27,28,29,30,31,16,17,18,..., dimensions={0} | all-to-all | bytes 1572864 | tf_op jit(solution)/shard_map/all_to_all | solution.py:128
  27.7 1.6 %shard_map.38 = (f32[16,1,384]{2,1,0:T(1,128)}, s32[1]{0:T(128)}) custom-call(bf16[384,1024]{1,0:T(8,128)(2,1)S(1)} %bitcast.14), custom_call_target="tpu_custom_call" | custom-call | tf_op jit(solution)/shard_map/pallas_call | solution.py:159
  29.3 5.2 %all-to-all-start.3 = ((f32[16,1,384]{2,1,0:T(1,128)}), f32[16,1,384]{2,1,0:T(1,128)S(1)}, u32[]{:S(2)}, u32[]{:S(2)}) async-start(f32[16,1,384]{2,1,0:T(1,128)} %get-tuple-element.44), calls=%async_computation.3 | async-start | bytes 49152 | tf_op jit(solution)/shard_map/all_to_all | solution.py:128
  35.2 3.6 %all-to-all-done.3 = f32[16,1,384]{2,1,0:T(1,128)S(1)} async-done(((f32[16,1,384]{2,1,0:T(1,128)}), f32[16,1,384]{2,1,0:T(1,128)S(1)}, u32[]{:S(2)}, u32[]{:S(2)}) %all-to-all-start.3) | async-done | bytes 24608 | tf_op jit(solution)/shard_map/all_to_all | solution.py:128
  38.8 0.0 copy-done
  38.8 0.0 copy-done.1
  38.8 0.0 copy-done.2
  38.9 0.9 %shard_map.39 = f32[1,256]{1,0:T(1,128)} custom-call(s32[1]{0:T(128)} %get-tuple-element.46.me_ref, f32[16,1,384]{2,1,0:T(1,128)S(1)} %get-tuple-element.47.best_ref, s32[2,256]{1,0:T(2,128)S(1)} %get-tuple-element.48.route_ref), custom_call_target="tpu_custom_call" | custom-call | tf_op jit(solution)/shard_map/pallas_call | solution.py:173
  (1 shorter events, 0.0 us)
Async XLA Ops:
  2.3 36.6 %copy-start = (bf16[256,1024]{1,0:T(8,128)(2,1)S(1)}, bf16[256,1024]{1,0:T(8,128)(2,1)}, u32[]{:S(2)}) copy-start(bf16[256,1024]{1,0:T(8,128)(2,1)} %x_hbm.1) | copy-start | bytes 1572868
  2.3 36.6 %copy-start.1 = (s32[256]{0:T(256)S(1)}, s32[256]{0:T(256)}, u32[]{:S(2)}) copy-start(s32[256]{0:T(256)} %param.8) | copy-start | bytes 3076
  2.3 36.6 %copy-start.2 = (s32[256]{0:T(256)S(1)}, s32[256]{0:T(256)}, u32[]{:S(2)}) copy-start(s32[256]{0:T(256)} %param.9) | copy-start | bytes 3076
  29.3 9.5 %all-to-all-start.3 = ((f32[16,1,384]{2,1,0:T(1,128)}), f32[16,1,384]{2,1,0:T(1,128)S(1)}, u32[]{:S(2)}, u32[]{:S(2)}) async-start(f32[16,1,384]{2,1,0:T(1,128)} %get-tuple-element.44), calls=%async_computation.3 | async-start | bytes 49152 | tf_op jit(solution)/shard_map/all_to_all | solution.py:128

commit v4 on v3

--- a/solution.py
+++ b/solution.py
@@ -31,13 +31,12 @@
 def pack_kernel(peers, rows, cap, spread_out, cl_hbm, od_hbm, x_hbm, out_ref, route_ref, cl_ref, od_ref, x_ref, sems):
     count, width = x_ref.shape
     step = 2 * LANES
-    pieces = [(cl_hbm, cl_ref), (od_hbm, od_ref)]
-    for k in range(width // step):
-        columns = pl.ds(k * step, step)
-        pieces.append((x_hbm.at[:, columns], x_ref.at[:, columns]))
+    pieces = [(cl_hbm, cl_ref), (od_hbm, od_ref), (x_hbm, x_ref)]
     copies = [pltpu.make_async_copy(src, dst, sems.at[k]) for k, (src, dst) in enumerate(pieces)]
     for copy in copies:
         copy.start()
+    before = (iota((count, count), 0) < iota((count, count), 1)).astype(jnp.bfloat16)
+    tag_row = (iota((peers * rows, peers), 0) == iota((peers * rows, peers), 1) * rows + cap).astype(jnp.bfloat16)
     copies[0].wait()
     copies[1].wait()
     cl = cl_ref[...]
@@ -49,7 +48,6 @@
         dest = cl >> (CL_DEV.bit_length() - 1)
         group = cl & (CL_DEV - 1)
     mine = iota((peers, count), 0) == dest
-    before = (iota((count, count), 0) < iota((count, count), 1)).astype(jnp.bfloat16)
     ahead = nn(mine.astype(jnp.bfloat16), before)
     rank = jnp.sum(jnp.where(mine, ahead, 0.0), axis=0, keepdims=True).astype(jnp.int32)
     route_ref[0:1, :] = dest
@@ -63,11 +61,10 @@
     ).astype(jnp.bfloat16)
     place = ((iota((LANES, count), 0) == rank) & fits).astype(jnp.bfloat16)
     tags = nt(spread, place).astype(jnp.bfloat16)
-    tag_row = (iota((peers * rows, peers), 0) == iota((peers * rows, peers), 1) * rows + cap).astype(jnp.bfloat16)
     crowded = jnp.max((rank >= cap).astype(jnp.float32), axis=1, keepdims=True)
     crowded = jnp.broadcast_to(crowded, (peers, LANES)).astype(jnp.bfloat16)
+    copies[2].wait()
     for k in range(width // step):
-        copies[2 + k].wait()
         part = nn(pick, x_ref[:, k * step:(k + 1) * step])
         if k == 0:
             part += nn(tag_row, jnp.concatenate([tags[0:peers], tags[peers:2 * peers]], axis=1))
@@ -103,7 +100,8 @@
     usable = (key_col < key) & (key_col >= floor)
     largest = jnp.max(jnp.where(usable, gram * scale_col, LOWEST), axis=0, keepdims=True)
     best = jnp.where(largest > LOWEST, jnp.maximum(largest * scale / width, -1.0), -1.0)
-    best_ref[...] = jnp.broadcast_to(best[None], best_ref.shape)
+    for peer in range(peers):
+        best_ref[peer] = best
 
 
 def take_kernel(rows, me_ref, best_ref, route_ref, out_ref):
@@ -124,13 +122,13 @@
 
 def exchange(blocks):
     peers = blocks.shape[0]
-    group = [(k + peers // 2 + 1) % peers for k in range(peers)]
+    group = [(k + peers // 2 + 3) % peers for k in range(peers)]
     return lax.all_to_all(blocks, "owner", split_axis=0, concat_axis=0, tiled=True, axis_index_groups=[group])
 
 
 def place_in_group():
     peers = lax.axis_size("owner")
-    return ((lax.axis_index("owner") + (peers - peers // 2 - 1)) % peers).astype(jnp.int32).reshape(1)
+    return ((lax.axis_index("owner") + (peers - peers // 2 - 3)) % peers).astype(jnp.int32).reshape(1)
 
 
 def send(rows, cap, spread_out, embeds, cluster, order):
@@ -151,7 +149,7 @@
             pltpu.VMEM((1, count), jnp.int32),
             pltpu.VMEM((1, count), jnp.int32),
             pltpu.VMEM((count, width), jnp.bfloat16),
-            pltpu.SemaphoreType.DMA((2 + width // (2 * LANES),)),
+            pltpu.SemaphoreType.DMA((3,)),
         ],
         compiler_params=PARAMS,
     )(cluster.reshape(1, count), order.reshape(1, count), embeds)

time: 40 us -> 38.5 us (0.963)
  starting transfers between devices: 5.24 us -> 6.23 us
  waiting for transfers between devices: 3.63 us -> 2.73 us
  blocking collectives: 25.5 us -> 24.6 us
  Pallas kernels: 4.68 us -> 3.98 us
    all_to_all x1, starting transfers between devices: 5.24 us -> 6.23 us  [exchange(): lax.all_to_all(blocks, 'owner', split_axis=0, concat_axis=0, tiled=True,...]
    all_to_all x1, waiting for transfers between devices: 3.63 us -> 2.73 us  [exchange(): lax.all_to_all(blocks, 'owner', split_axis=0, concat_axis=0, tiled=True,...]
    all_to_all x1, blocking collectives: 25.5 us -> 24.6 us  [exchange(): lax.all_to_all(blocks, 'owner', split_axis=0, concat_axis=0, tiled=True,...]
    pallas_call x1, Pallas kernels: 2.24 us -> 1.54 us  [send(): pl.pallas_call(functools.partial(pack_kernel, peers, rows, cap, spread_ou...]
where the time goes in v4:
time: 38.5 us; the launch traced here: 38.3 us
  blocking collectives  24.6 us (64%)
  starting transfers between devices  6.23 us (16%)
  Pallas kernels  3.98 us (10%)
  waiting for transfers between devices  2.73 us (7%)
  between operations  0.71 us (2%)
    all_to_all x1, blocking collectives, exchange(): lax.all_to_all(blocks, 'owner', split_axis=0, concat_axis=0, tiled=True,...  24.6 us
    all_to_all x1, starting transfers between devices, exchange(): lax.all_to_all(blocks, 'owner', split_axis=0, concat_axis=0, tiled=True,...  6.23 us
    all_to_all x1, waiting for transfers between devices, exchange(): lax.all_to_all(blocks, 'owner', split_axis=0, concat_axis=0, tiled=True,...  2.73 us
    pallas_call x1, Pallas kernels, send(): pl.pallas_call(functools.partial(best_kernel, peers, rows, cap), out_shap...  1.56 us
    pallas_call x1, Pallas kernels, send(): pl.pallas_call(functools.partial(pack_kernel, peers, rows, cap, spread_ou...  1.54 us
    pallas_call x1, Pallas kernels, take(): pl.pallas_call(functools.partial(take_kernel, rows), out_shape=jax.ShapeD...  0.88 us
  transfers between devices with their start and end apart: 1, of which 1 were waited for; matrix products, arithmetic and copies ran while one was open for 0% of the time, Pallas kernels for 0%

profile of v4, /device:TPU:0, one launch (start us, length us, event | category | flops | bytes accessed | tf_op | source)
XLA Modules:
  0.0 38.3 jit_solution(7275588145453011894)
XLA Ops:
  0.0 1.5 %shard_map.37 = (bf16[384,1024]{1,0:T(8,128)(2,1)S(1)}, s32[2,256]{1,0:T(2,128)S(1)}) custom-call(s32[1,256]{1,0:T(1,128)} %bitcast.18, s32[1,256]{1,0:T(1,128)} %bitcast.20, bf16[256,1024]{1,0:T(8,128)(2,1)} %x_hbm.1), custom_call_target="tpu_custom_call" | custom-call | tf_op jit(solution)/shard_map/pallas_call | solution.py:140
  1.6 0.0 copy-start
  1.6 0.0 copy-start.1
  1.6 0.0 copy-start.2
  1.6 24.6 %all_to_all.19 = bf16[16,24,1024]{2,1,0:T(8,128)(2,1)S(1)} all-to-all(bf16[16,24,1024]{2,1,0:T(8,128)(2,1)S(1)} %bitcast.16), channel_id=1, replica_groups={{11,12,13,14,15,0,1,2,3,4,5,6,7,8,9,10},{27,28,29,30,31,16,17,18,19,20,..., dimensions={0} | all-to-all | bytes 1572864 | tf_op jit(solution)/shard_map/all_to_all | solution.py:126
  26.2 1.6 %shard_map.38 = (f32[16,1,384]{2,1,0:T(1,128)}, s32[1]{0:T(128)}) custom-call(bf16[384,1024]{1,0:T(8,128)(2,1)S(1)} %bitcast.14), custom_call_target="tpu_custom_call" | custom-call | tf_op jit(solution)/shard_map/pallas_call | solution.py:157
  27.7 6.2 %all-to-all-start.3 = ((f32[16,1,384]{2,1,0:T(1,128)}), f32[16,1,384]{2,1,0:T(1,128)S(1)}, u32[]{:S(2)}, u32[]{:S(2)}) async-start(f32[16,1,384]{2,1,0:T(1,128)} %get-tuple-element.44), calls=%async_computation.3 | async-start | bytes 49152 | tf_op jit(solution)/shard_map/all_to_all | solution.py:126
  34.6 2.7 %all-to-all-done.3 = f32[16,1,384]{2,1,0:T(1,128)S(1)} async-done(((f32[16,1,384]{2,1,0:T(1,128)}), f32[16,1,384]{2,1,0:T(1,128)S(1)}, u32[]{:S(2)}, u32[]{:S(2)}) %all-to-all-start.3) | async-done | bytes 24608 | tf_op jit(solution)/shard_map/all_to_all | solution.py:126
  37.4 0.0 copy-done
  37.4 0.0 copy-done.1
  37.4 0.0 copy-done.2
  37.4 0.9 %shard_map.39 = f32[1,256]{1,0:T(1,128)} custom-call(s32[1]{0:T(128)} %get-tuple-element.46.me_ref, f32[16,1,384]{2,1,0:T(1,128)S(1)} %get-tuple-element.47.best_ref, s32[2,256]{1,0:T(2,128)S(1)} %get-tuple-element.48.route_ref), custom_call_target="tpu_custom_call" | custom-call | tf_op jit(solution)/shard_map/pallas_call | solution.py:171
  (1 shorter events, 0.0 us)
Async XLA Ops:
  1.6 35.8 %copy-start = (bf16[256,1024]{1,0:T(8,128)(2,1)S(1)}, bf16[256,1024]{1,0:T(8,128)(2,1)}, u32[]{:S(2)}) copy-start(bf16[256,1024]{1,0:T(8,128)(2,1)} %x_hbm.1) | copy-start | bytes 1572868
  1.6 35.8 %copy-start.1 = (s32[256]{0:T(256)S(1)}, s32[256]{0:T(256)}, u32[]{:S(2)}) copy-start(s32[256]{0:T(256)} %param.8) | copy-start | bytes 3076
  1.6 35.8 %copy-start.2 = (s32[256]{0:T(256)S(1)}, s32[256]{0:T(256)}, u32[]{:S(2)}) copy-start(s32[256]{0:T(256)} %param.9) | copy-start | bytes 3076
  27.7 9.6 %all-to-all-start.3 = ((f32[16,1,384]{2,1,0:T(1,128)}), f32[16,1,384]{2,1,0:T(1,128)S(1)}, u32[]{:S(2)}, u32[]{:S(2)}) async-start(f32[16,1,384]{2,1,0:T(1,128)} %get-tuple-element.44), calls=%async_computation.3 | async-start | bytes 49152 | tf_op jit(solution)/shard_map/all_to_all | solution.py:126

commit v5 on v4

--- a/solution.py
+++ b/solution.py
@@ -26,6 +26,19 @@
 
 def nn(a, b):
     return lax.dot_general(a, b, (((1,), (0,)), ((), ())), preferred_element_type=jnp.float32)
+
+
+def parts(values):
+    high = values.astype(jnp.bfloat16)
+    rest = values - high.astype(jnp.float32)
+    mid = rest.astype(jnp.bfloat16)
+    low = (rest - mid.astype(jnp.float32)).astype(jnp.bfloat16)
+    return jnp.concatenate([high, mid, low], axis=0)
+
+
+def whole(sums):
+    third = sums.shape[0] // 3
+    return sums[:third] + sums[third:2 * third] + sums[2 * third:]
 
 
 def pack_kernel(peers, rows, cap, spread_out, cl_hbm, od_hbm, x_hbm, out_ref, route_ref, cl_ref, od_ref, x_ref, sems):
@@ -100,23 +113,16 @@
     usable = (key_col < key) & (key_col >= floor)
     largest = jnp.max(jnp.where(usable, gram * scale_col, LOWEST), axis=0, keepdims=True)
     best = jnp.where(largest > LOWEST, jnp.maximum(largest * scale / width, -1.0), -1.0)
-    for peer in range(peers):
-        best_ref[peer] = best
-
-
-def take_kernel(rows, me_ref, best_ref, route_ref, out_ref):
-    peers, _, total = best_ref.shape
+    shares = nt(parts(jnp.where(block, best, 0.0)), spread)
+    best_ref[:, 0, :] = whole(shares)
+
+
+def take_kernel(best_ref, route_ref, out_ref):
+    peers, _, most = best_ref.shape
     count = out_ref.shape[1]
-    dest = route_ref[0:1, :]
-    slot = me_ref[0] * rows + route_ref[1:2, :]
-    best = best_ref[:, 0, :]
-    high = best.astype(jnp.bfloat16)
-    rest = best - high.astype(jnp.float32)
-    mid = rest.astype(jnp.bfloat16)
-    low = (rest - mid.astype(jnp.float32)).astype(jnp.bfloat16)
-    pick = (iota((total, count), 0) == slot).astype(jnp.bfloat16)
-    found = nn(high, pick) + nn(mid, pick) + nn(low, pick)
-    mine = iota((peers, count), 0) == dest
+    pick = (iota((most, count), 0) == route_ref[1:2, :]).astype(jnp.bfloat16)
+    found = whole(nn(parts(best_ref[:, 0, :]), pick))
+    mine = iota((peers, count), 0) == route_ref[0:1, :]
     out_ref[...] = jnp.sum(jnp.where(mine, found, 0.0), axis=0, keepdims=True)
 
 
@@ -124,11 +130,6 @@
     peers = blocks.shape[0]
     group = [(k + peers // 2 + 3) % peers for k in range(peers)]
     return lax.all_to_all(blocks, "owner", split_axis=0, concat_axis=0, tiled=True, axis_index_groups=[group])
-
-
-def place_in_group():
-    peers = lax.axis_size("owner")
-    return ((lax.axis_index("owner") + (peers - peers // 2 - 3)) % peers).astype(jnp.int32).reshape(1)
 
 
 def send(rows, cap, spread_out, embeds, cluster, order):
@@ -156,7 +157,7 @@
     arrived = exchange(packed.reshape(peers, rows, width))
     best, crowded = pl.pallas_call(
         functools.partial(best_kernel, peers, rows, cap),
-        out_shape=[jax.ShapeDtypeStruct((peers, 1, total), jnp.float32), jax.ShapeDtypeStruct((1,), jnp.int32)],
+        out_shape=[jax.ShapeDtypeStruct((peers, 1, LANES), jnp.float32), jax.ShapeDtypeStruct((1,), jnp.int32)],
         in_specs=[vmem],
         out_specs=[vmem, smem],
         compiler_params=PARAMS,
@@ -164,17 +165,16 @@
     return best, route, crowded
 
 
-def take(rows, me, returned, route):
+def take(returned, route):
     count = route.shape[1]
     vmem = pl.BlockSpec(memory_space=pltpu.VMEM)
-    smem = pl.BlockSpec(memory_space=pltpu.SMEM)
     nearest = pl.pallas_call(
-        functools.partial(take_kernel, rows),
+        take_kernel,
         out_shape=jax.ShapeDtypeStruct((1, count), jnp.float32),
-        in_specs=[smem, vmem, vmem],
+        in_specs=[vmem] * 2,
         out_specs=vmem,
         compiler_params=PARAMS,
-    )(me, returned, route)
+    )(returned, route)
     return nearest.reshape(count)
 
 
@@ -185,7 +185,7 @@
     def roomy():
         rows = -(-(most + 1) // 8) * 8
         best, route, _ = send(rows, most, False, embeds, cluster, order)
-        return take(rows, place_in_group(), exchange(best), route)
+        return take(exchange(best), route)
 
     rows = 3 * most // 4
     if rows % 8:
@@ -194,11 +194,12 @@
     returned = exchange(best)
 
     def again():
-        results = jnp.zeros_like(returned).at[0, 0, :count].set(roomy())
-        places = jnp.stack([jnp.zeros((count,), jnp.int32), jnp.arange(count, dtype=jnp.int32)])
-        return jnp.zeros((1,), jnp.int32), results, places
-
-    return take(rows, *lax.cond(crowded[0] > 0, again, lambda: (place_in_group(), returned, route)))
+        table = roomy().reshape(-1, LANES)
+        results = jnp.zeros_like(returned).at[: table.shape[0], 0].set(table)
+        row = jnp.arange(count, dtype=jnp.int32)
+        return results, jnp.stack([row // LANES, row % LANES])
+
+    return take(*lax.cond(crowded[0] > 0, again, lambda: (returned, route)))
 
 
 def solution(mesh):

time: 38.5 us -> 38.3 us (level)
  no operation moved by 1% of the time
where the time goes in v5:
time: 38.3 us; the launch traced here: 38 us
  blocking collectives  24.6 us (64%)
  starting transfers between devices  6.21 us (16%)
  Pallas kernels  3.94 us (10%)
  waiting for transfers between devices  2.57 us (7%)
  between operations  0.71 us (2%)
    all_to_all x1, blocking collectives, exchange(): lax.all_to_all(blocks, 'owner', split_axis=0, concat_axis=0, tiled=True,...  24.6 us
    all_to_all x1, starting transfers between devices, exchange(): lax.all_to_all(blocks, 'owner', split_axis=0, concat_axis=0, tiled=True,...  6.21 us
    all_to_all x1, waiting for transfers between devices, exchange(): lax.all_to_all(blocks, 'owner', split_axis=0, concat_axis=0, tiled=True,...  2.57 us
    pallas_call x1, Pallas kernels, send(): pl.pallas_call(functools.partial(best_kernel, peers, rows, cap), out_shap...  1.66 us
    pallas_call x1, Pallas kernels, send(): pl.pallas_call(functools.partial(pack_kernel, peers, rows, cap, spread_ou...  1.54 us
  transfers between devices with their start and end apart: 1, of which 1 were waited for; matrix products, arithmetic and copies ran while one was open for 0% of the time, Pallas kernels for 0%

profile of v5, /device:TPU:0, one launch (start us, length us, event | category | flops | bytes accessed | tf_op | source)
XLA Modules:
  0.0 38.0 jit_solution(6767665904926312788)
XLA Ops:
  0.0 1.5 %shard_map.37 = (bf16[384,1024]{1,0:T(8,128)(2,1)S(1)}, s32[2,256]{1,0:T(2,128)S(1)}) custom-call(s32[1,256]{1,0:T(1,128)} %bitcast.20, s32[1,256]{1,0:T(1,128)} %bitcast.22, bf16[256,1024]{1,0:T(8,128)(2,1)} %x_hbm.1), custom_call_target="tpu_custom_call" | custom-call | tf_op jit(solution)/shard_map/pallas_call | solution.py:141
  1.6 0.0 copy-start
  1.6 0.0 copy-start.1
  1.6 0.0 copy-start.2
  1.6 24.6 %all_to_all.18 = bf16[16,24,1024]{2,1,0:T(8,128)(2,1)S(1)} all-to-all(bf16[16,24,1024]{2,1,0:T(8,128)(2,1)S(1)} %bitcast.17), channel_id=1, replica_groups={{11,12,13,14,15,0,1,2,3,4,5,6,7,8,9,10},{27,28,29,30,31,16,17,18,19,20,..., dimensions={0} | all-to-all | bytes 1572864 | tf_op jit(solution)/shard_map/all_to_all | solution.py:132
  26.2 1.7 %shard_map.38 = (f32[16,1,128]{2,1,0:T(1,128)}, s32[1]{0:T(128)}) custom-call(bf16[384,1024]{1,0:T(8,128)(2,1)S(1)} %bitcast.16), custom_call_target="tpu_custom_call" | custom-call | tf_op jit(solution)/shard_map/pallas_call | solution.py:158
  27.8 6.2 %all-to-all-start.3 = ((f32[16,1,128]{2,1,0:T(1,128)}), f32[16,1,128]{2,1,0:T(1,128)S(1)}, u32[]{:S(2)}, u32[]{:S(2)}) async-start(f32[16,1,128]{2,1,0:T(1,128)} %get-tuple-element.41), calls=%async_computation.3 | async-start | bytes 16384 | tf_op jit(solution)/shard_map/all_to_all | solution.py:132
  34.7 2.6 %all-to-all-done.3 = f32[16,1,128]{2,1,0:T(1,128)S(1)} async-done(((f32[16,1,128]{2,1,0:T(1,128)}), f32[16,1,128]{2,1,0:T(1,128)S(1)}, u32[]{:S(2)}, u32[]{:S(2)}) %all-to-all-start.3) | async-done | bytes 8224 | tf_op jit(solution)/shard_map/all_to_all | solution.py:132
  37.3 0.0 copy-done
  37.3 0.0 copy-done.1
  37.3 0.0 copy-done.2
  37.3 0.7 %shard_map.39 = f32[1,256]{1,0:T(1,128)} custom-call(f32[16,1,128]{2,1,0:T(1,128)S(1)} %get-tuple-element.47.best_ref, s32[2,256]{1,0:T(2,128)S(1)} %get-tuple-element.44.route_ref), custom_call_target="tpu_custom_call" | custom-call | tf_op jit(solution)/shard_map/pallas_call | solution.py:171
  (1 shorter events, 0.0 us)
Async XLA Ops:
  1.6 35.7 %copy-start = (bf16[256,1024]{1,0:T(8,128)(2,1)S(1)}, bf16[256,1024]{1,0:T(8,128)(2,1)}, u32[]{:S(2)}) copy-start(bf16[256,1024]{1,0:T(8,128)(2,1)} %x_hbm.1) | copy-start | bytes 1572868
  1.6 35.7 %copy-start.1 = (s32[256]{0:T(256)S(1)}, s32[256]{0:T(256)}, u32[]{:S(2)}) copy-start(s32[256]{0:T(256)} %param.8) | copy-start | bytes 3076
  1.6 35.7 %copy-start.2 = (s32[256]{0:T(256)S(1)}, s32[256]{0:T(256)}, u32[]{:S(2)}) copy-start(s32[256]{0:T(256)} %param.9) | copy-start | bytes 3076
  27.8 9.4 %all-to-all-start.3 = ((f32[16,1,128]{2,1,0:T(1,128)}), f32[16,1,128]{2,1,0:T(1,128)S(1)}, u32[]{:S(2)}, u32[]{:S(2)}) async-start(f32[16,1,128]{2,1,0:T(1,128)} %get-tuple-element.41), calls=%async_computation.3 | async-start | bytes 16384 | tf_op jit(solution)/shard_map/all_to_all | solution.py:132

commit v6 on v5

--- a/solution.py
+++ b/solution.py
@@ -77,7 +77,7 @@
     crowded = jnp.max((rank >= cap).astype(jnp.float32), axis=1, keepdims=True)
     crowded = jnp.broadcast_to(crowded, (peers, LANES)).astype(jnp.bfloat16)
     copies[2].wait()
-    for k in range(width // step):
+    for k in reversed(range(width // step)):
         part = nn(pick, x_ref[:, k * step:(k + 1) * step])
         if k == 0:
             part += nn(tag_row, jnp.concatenate([tags[0:peers], tags[peers:2 * peers]], axis=1))
@@ -91,7 +91,7 @@
     gram = nt(x_ref[...], x_ref[...])
     tag_row = (iota((peers, total), 1) == iota((peers, total), 0) * rows + cap).astype(jnp.bfloat16)
     tags = nn(tag_row, x_ref[:, :4 * LANES])
-    crowded_ref[0] = jnp.max(tags[:, 3 * LANES:]).astype(jnp.int32)
+    crowded_ref[...] = jnp.max(tags[:, 3 * LANES:], axis=0, keepdims=True)
     cols = iota((peers, total), 1)
     first = iota((peers, total), 0) * rows
     block = (cols >= first) & (cols < first + rows)
@@ -128,7 +128,7 @@
 
 def exchange(blocks):
     peers = blocks.shape[0]
-    group = [(k + peers // 2 + 3) % peers for k in range(peers)]
+    group = [k ^ (peers // 2 + 3) for k in range(peers)]
     return lax.all_to_all(blocks, "owner", split_axis=0, concat_axis=0, tiled=True, axis_index_groups=[group])
 
 
@@ -137,7 +137,6 @@
     peers = lax.axis_size("owner")
     total = peers * rows
     vmem = pl.BlockSpec(memory_space=pltpu.VMEM)
-    smem = pl.BlockSpec(memory_space=pltpu.SMEM)
     packed, route = pl.pallas_call(
         functools.partial(pack_kernel, peers, rows, cap, spread_out),
         out_shape=[
@@ -157,9 +156,9 @@
     arrived = exchange(packed.reshape(peers, rows, width))
     best, crowded = pl.pallas_call(
         functools.partial(best_kernel, peers, rows, cap),
-        out_shape=[jax.ShapeDtypeStruct((peers, 1, LANES), jnp.float32), jax.ShapeDtypeStruct((1,), jnp.int32)],
+        out_shape=[jax.ShapeDtypeStruct((peers, 1, LANES), jnp.float32), jax.ShapeDtypeStruct((1, LANES), jnp.float32)],
         in_specs=[vmem],
-        out_specs=[vmem, smem],
+        out_specs=[vmem, vmem],
         compiler_params=PARAMS,
     )(arrived.reshape(total, width))
     return best, route, crowded
@@ -199,7 +198,7 @@
         row = jnp.arange(count, dtype=jnp.int32)
         return results, jnp.stack([row // LANES, row % LANES])
 
-    return take(*lax.cond(crowded[0] > 0, again, lambda: (returned, route)))
+    return take(*lax.cond(crowded[0, 0] > 0, again, lambda: (returned, route)))
 
 
 def solution(mesh):

time: 38.3 us -> 38 us (level)
  between operations: 0.71 us -> 0.09 us
  waiting for transfers between devices: 2.57 us -> 3.1 us
  starting transfers between devices: 6.21 us -> 5.81 us
    all_to_all x1, waiting for transfers between devices: 2.57 us -> 3.1 us  [exchange(): lax.all_to_all(blocks, 'owner', split_axis=0, concat_axis=0, tiled=True,...]
    all_to_all x1, starting transfers between devices: 6.21 us -> 5.81 us  [exchange(): lax.all_to_all(blocks, 'owner', split_axis=0, concat_axis=0, tiled=True,...]
where the time goes in v6:
time: 38 us; the launch traced here: 37.8 us
  blocking collectives  24.8 us (65%)
  starting transfers between devices  5.81 us (15%)
  Pallas kernels  3.96 us (10%)
  waiting for transfers between devices  3.1 us (8%)
    all_to_all x1, blocking collectives, exchange(): lax.all_to_all(blocks, 'owner', split_axis=0, concat_axis=0, tiled=True,...  24.8 us
    all_to_all x1, starting transfers between devices, exchange(): lax.all_to_all(blocks, 'owner', split_axis=0, concat_axis=0, tiled=True,...  5.81 us
    all_to_all x1, waiting for transfers between devices, exchange(): lax.all_to_all(blocks, 'owner', split_axis=0, concat_axis=0, tiled=True,...  3.1 us
    pallas_call x1, Pallas kernels, send(): pl.pallas_call(functools.partial(best_kernel, peers, rows, cap), out_shap...  1.65 us
    pallas_call x1, Pallas kernels, send(): pl.pallas_call(functools.partial(pack_kernel, peers, rows, cap, spread_ou...  1.57 us
  transfers between devices with their start and end apart: 1, of which 1 were waited for; matrix products, arithmetic and copies ran while one was open for 0% of the time, Pallas kernels for 0%

profile of v6, /device:TPU:0, one launch (start us, length us, event | category | flops | bytes accessed | tf_op | source)
XLA Modules:
  0.0 37.8 jit_solution(9805049258650234177)
XLA Ops:
  0.0 1.6 %shard_map.37 = (bf16[384,1024]{1,0:T(8,128)(2,1)S(1)}, s32[2,256]{1,0:T(2,128)S(1)}) custom-call(s32[1,256]{1,0:T(1,128)} %bitcast.22, s32[1,256]{1,0:T(1,128)} %bitcast.24, bf16[256,1024]{1,0:T(8,128)(2,1)} %x_hbm.1), custom_call_target="tpu_custom_call" | custom-call | tf_op jit(solution)/shard_map/pallas_call | solution.py:140
  1.6 0.0 copy-start
  1.6 0.0 copy-start.1
  1.6 0.0 copy-start.2
  1.6 24.8 %all_to_all.18 = bf16[16,24,1024]{2,1,0:T(8,128)(2,1)S(1)} all-to-all(bf16[16,24,1024]{2,1,0:T(8,128)(2,1)S(1)} %bitcast.18), channel_id=1, replica_groups={{11,10,9,8,15,14,13,12,3,2,1,0,7,6,5,4},{27,26,25,24,31,30,29,28,19,18,..., dimensions={0} | all-to-all | bytes 1572864 | tf_op jit(solution)/shard_map/all_to_all | solution.py:132
  26.4 1.7 %shard_map.38 = (f32[16,1,128]{2,1,0:T(1,128)}, f32[1,128]{1,0:T(1,128)S(1)}) custom-call(bf16[384,1024]{1,0:T(8,128)(2,1)S(1)} %bitcast.17), custom_call_target="tpu_custom_call" | custom-call | tf_op jit(solution)/shard_map/pallas_call | solution.py:157
  28.1 5.8 %all-to-all-start.3 = ((f32[16,1,128]{2,1,0:T(1,128)}), f32[16,1,128]{2,1,0:T(1,128)S(1)}, u32[]{:S(2)}, u32[]{:S(2)}) async-start(f32[16,1,128]{2,1,0:T(1,128)} %get-tuple-element.41), calls=%async_computation.3 | async-start | bytes 16384 | tf_op jit(solution)/shard_map/all_to_all | solution.py:132
  33.9 3.1 %all-to-all-done.3 = f32[16,1,128]{2,1,0:T(1,128)S(1)} async-done(((f32[16,1,128]{2,1,0:T(1,128)}), f32[16,1,128]{2,1,0:T(1,128)S(1)}, u32[]{:S(2)}, u32[]{:S(2)}) %all-to-all-start.3) | async-done | bytes 8224 | tf_op jit(solution)/shard_map/all_to_all | solution.py:132
  37.0 0.0 copy-done
  37.0 0.0 copy-done.1
  37.0 0.0 copy-done.2
  37.1 0.7 %shard_map.39 = f32[1,256]{1,0:T(1,128)} custom-call(f32[16,1,128]{2,1,0:T(1,128)S(1)} %get-tuple-element.47.best_ref, s32[2,256]{1,0:T(2,128)S(1)} %get-tuple-element.44.route_ref), custom_call_target="tpu_custom_call" | custom-call | tf_op jit(solution)/shard_map/pallas_call | solution.py:170
  (1 shorter events, 0.0 us)
Async XLA Ops:
  1.6 35.4 %copy-start = (bf16[256,1024]{1,0:T(8,128)(2,1)S(1)}, bf16[256,1024]{1,0:T(8,128)(2,1)}, u32[]{:S(2)}) copy-start(bf16[256,1024]{1,0:T(8,128)(2,1)} %x_hbm.1) | copy-start | bytes 1572868
  1.6 35.4 %copy-start.1 = (s32[256]{0:T(256)S(1)}, s32[256]{0:T(256)}, u32[]{:S(2)}) copy-start(s32[256]{0:T(256)} %param.8) | copy-start | bytes 3076
  1.6 35.4 %copy-start.2 = (s32[256]{0:T(256)S(1)}, s32[256]{0:T(256)}, u32[]{:S(2)}) copy-start(s32[256]{0:T(256)} %param.9) | copy-start | bytes 3076
  28.1 9.0 %all-to-all-start.3 = ((f32[16,1,128]{2,1,0:T(1,128)}), f32[16,1,128]{2,1,0:T(1,128)S(1)}, u32[]{:S(2)}, u32[]{:S(2)}) async-start(f32[16,1,128]{2,1,0:T(1,128)} %get-tuple-element.41), calls=%async_computation.3 | async-start | bytes 16384 | tf_op jit(solution)/shard_map/all_to_all | solution.py:132

commit v7 on v6

--- a/solution.py
+++ b/solution.py
@@ -43,7 +43,7 @@
 
 def pack_kernel(peers, rows, cap, spread_out, cl_hbm, od_hbm, x_hbm, out_ref, route_ref, cl_ref, od_ref, x_ref, sems):
     count, width = x_ref.shape
-    step = 2 * LANES
+    step = 4 * LANES
     pieces = [(cl_hbm, cl_ref), (od_hbm, od_ref), (x_hbm, x_ref)]
     copies = [pltpu.make_async_copy(src, dst, sems.at[k]) for k, (src, dst) in enumerate(pieces)]
     for copy in copies:
@@ -80,9 +80,8 @@
     for k in reversed(range(width // step)):
         part = nn(pick, x_ref[:, k * step:(k + 1) * step])
         if k == 0:
-            part += nn(tag_row, jnp.concatenate([tags[0:peers], tags[peers:2 * peers]], axis=1))
-        if k == 1:
-            part += nn(tag_row, jnp.concatenate([tags[2 * peers:], crowded], axis=1))
+            fields = [tags[f * peers:(f + 1) * peers] for f in range(3)]
+            part += nn(tag_row, jnp.concatenate([*fields, crowded], axis=1))
         out_ref[:, k * step:(k + 1) * step] = part.astype(jnp.bfloat16)
 
 

time: 38 us -> 38 us (level)
  no operation moved by 1% of the time
where the time goes in v7:
time: 38 us; the launch traced here: 37.8 us
  blocking collectives  24.8 us (65%)
  starting transfers between devices  5.81 us (15%)
  Pallas kernels  3.96 us (10%)
  waiting for transfers between devices  3.1 us (8%)
    all_to_all x1, blocking collectives, exchange(): lax.all_to_all(blocks, 'owner', split_axis=0, concat_axis=0, tiled=True,...  24.8 us
    all_to_all x1, starting transfers between devices, exchange(): lax.all_to_all(blocks, 'owner', split_axis=0, concat_axis=0, tiled=True,...  5.81 us
    all_to_all x1, waiting for transfers between devices, exchange(): lax.all_to_all(blocks, 'owner', split_axis=0, concat_axis=0, tiled=True,...  3.1 us
    pallas_call x1, Pallas kernels, send(): pl.pallas_call(functools.partial(best_kernel, peers, rows, cap), out_shap...  1.65 us
    pallas_call x1, Pallas kernels, send(): pl.pallas_call(functools.partial(pack_kernel, peers, rows, cap, spread_ou...  1.57 us
  transfers between devices with their start and end apart: 1, of which 1 were waited for; matrix products, arithmetic and copies ran while one was open for 0% of the time, Pallas kernels for 0%

profile of v7, /device:TPU:0, one launch (start us, length us, event | category | flops | bytes accessed | tf_op | source)
XLA Modules:
  0.0 37.8 jit_solution(4218687289707321658)
XLA Ops:
  0.0 1.6 %shard_map.37 = (bf16[384,1024]{1,0:T(8,128)(2,1)S(1)}, s32[2,256]{1,0:T(2,128)S(1)}) custom-call(s32[1,256]{1,0:T(1,128)} %bitcast.22, s32[1,256]{1,0:T(1,128)} %bitcast.24, bf16[256,1024]{1,0:T(8,128)(2,1)} %x_hbm.1), custom_call_target="tpu_custom_call" | custom-call | tf_op jit(solution)/shard_map/pallas_call | solution.py:139
  1.6 0.0 copy-start
  1.6 0.0 copy-start.1
  1.6 0.0 copy-start.2
  1.6 24.8 %all_to_all.18 = bf16[16,24,1024]{2,1,0:T(8,128)(2,1)S(1)} all-to-all(bf16[16,24,1024]{2,1,0:T(8,128)(2,1)S(1)} %bitcast.18), channel_id=1, replica_groups={{11,10,9,8,15,14,13,12,3,2,1,0,7,6,5,4},{27,26,25,24,31,30,29,28,19,18,..., dimensions={0} | all-to-all | bytes 1572864 | tf_op jit(solution)/shard_map/all_to_all | solution.py:131
  26.4 1.7 %shard_map.38 = (f32[16,1,128]{2,1,0:T(1,128)}, f32[1,128]{1,0:T(1,128)S(1)}) custom-call(bf16[384,1024]{1,0:T(8,128)(2,1)S(1)} %bitcast.17), custom_call_target="tpu_custom_call" | custom-call | tf_op jit(solution)/shard_map/pallas_call | solution.py:156
  28.1 5.8 %all-to-all-start.3 = ((f32[16,1,128]{2,1,0:T(1,128)}), f32[16,1,128]{2,1,0:T(1,128)S(1)}, u32[]{:S(2)}, u32[]{:S(2)}) async-start(f32[16,1,128]{2,1,0:T(1,128)} %get-tuple-element.41), calls=%async_computation.3 | async-start | bytes 16384 | tf_op jit(solution)/shard_map/all_to_all | solution.py:131
  33.9 3.1 %all-to-all-done.3 = f32[16,1,128]{2,1,0:T(1,128)S(1)} async-done(((f32[16,1,128]{2,1,0:T(1,128)}), f32[16,1,128]{2,1,0:T(1,128)S(1)}, u32[]{:S(2)}, u32[]{:S(2)}) %all-to-all-start.3) | async-done | bytes 8224 | tf_op jit(solution)/shard_map/all_to_all | solution.py:131
  37.0 0.0 copy-done
  37.0 0.0 copy-done.1
  37.0 0.0 copy-done.2
  37.0 0.7 %shard_map.39 = f32[1,256]{1,0:T(1,128)} custom-call(f32[16,1,128]{2,1,0:T(1,128)S(1)} %get-tuple-element.47.best_ref, s32[2,256]{1,0:T(2,128)S(1)} %get-tuple-element.44.route_ref), custom_call_target="tpu_custom_call" | custom-call | tf_op jit(solution)/shard_map/pallas_call | solution.py:169
  (1 shorter events, 0.0 us)
Async XLA Ops:
  1.6 35.4 %copy-start = (bf16[256,1024]{1,0:T(8,128)(2,1)S(1)}, bf16[256,1024]{1,0:T(8,128)(2,1)}, u32[]{:S(2)}) copy-start(bf16[256,1024]{1,0:T(8,128)(2,1)} %x_hbm.1) | copy-start | bytes 1572868
  1.6 35.4 %copy-start.1 = (s32[256]{0:T(256)S(1)}, s32[256]{0:T(256)}, u32[]{:S(2)}) copy-start(s32[256]{0:T(256)} %param.8) | copy-start | bytes 3076
  1.6 35.4 %copy-start.2 = (s32[256]{0:T(256)S(1)}, s32[256]{0:T(256)}, u32[]{:S(2)}) copy-start(s32[256]{0:T(256)} %param.9) | copy-start | bytes 3076
  28.1 9.0 %all-to-all-start.3 = ((f32[16,1,128]{2,1,0:T(1,128)}), f32[16,1,128]{2,1,0:T(1,128)S(1)}, u32[]{:S(2)}, u32[]{:S(2)}) async-start(f32[16,1,128]{2,1,0:T(1,128)} %get-tuple-element.41), calls=%async_computation.3 | async-start | bytes 16384 | tf_op jit(solution)/shard_map/all_to_all | solution.py:131
